TPU v7x, 32 devices: a whole 2x2x4 slice. The times are simulated.
32 devices in a mesh: sta: 8 (over y, x, core), tm: 4 (over z).
Axes of the slice: x: 2, y: 2, z: 4, core: 2. Of those that a mesh axis runs over, the one named last changes fastest.
Arguments:
- records: bfloat16 [8, 3, 2048], P('sta', None, 'tm'), may hold values from -700 to 700
- templates: bfloat16 [8, 3, 256, 300], P('sta', None, 'tm'), may hold values from -80 to 80
- channel_mask: int32 [8, 3, 256], P('sta', None, 'tm'), may hold values 0 or 1
- moveouts: int32 [8, 256], P('sta'), may hold values from 0 to 200, as said below
Outputs:
- stack: float32 [256, 2048], P('sta', 'tm')
Inputs may be any that keep to these rules, and one draw needn't show every extreme that they name: `moveouts`: for each template the smallest moveout over all stations is 0 and the largest is 200.
All inputs are finite; a program needn't handle non-finite values. No bound on the sum of `channel_mask` on one device may be relied on, other than what follows from the above.
Results may differ from a plain program's by a relative error of at most 0.0032.
Values may be sent and summed in bfloat16 or wider, within the bound.
No kernel may reach another device: no remote copies, remote signals or barrier semaphores. Data moves between devices by JAX's collectives and lax.ppermute only.
A program may use at most 64 MiB of HBM per device.

v0:
```python
import functools
import jax
import jax.numpy as jnp
from jax import lax
from jax.experimental import pallas as pl
from jax.experimental.pallas import tpu as pltpu
from jax.sharding import PartitionSpec as P

TAPS = 300
MAX_MOVEOUT = 200
TAPS_PAD = 384
LANES = 128
F32 = jnp.float32
BF16 = jnp.bfloat16


def column_of(row, rows):
    n = row.shape[1]
    wide = jnp.broadcast_to(row, (rows, n))
    at = lax.broadcasted_iota(jnp.int32, (rows, n), 0) == lax.broadcasted_iota(jnp.int32, (rows, n), 1)
    return jnp.sum(jnp.where(at, wide, jnp.zeros_like(wide)), axis=1, keepdims=True)


def shape_kernel(templates_ref, mask_ref, shaped_ref):
    rows = templates_ref.shape[1]
    for c in range(3):
        values = templates_ref[c].astype(F32)
        center = jnp.sum(values, axis=1, keepdims=True) / TAPS
        spread = values - center
        rms = jnp.sqrt(jnp.sum(spread * spread, axis=1, keepdims=True) / TAPS + 1e-06)
        weight = column_of(mask_ref[c : c + 1, :].astype(F32), rows)
        shaped = (spread / rms * weight).astype(BF16)
        shaped_ref[c, :, 0:256] = shaped[:, 0:256]
        tail = jnp.concatenate([shaped[:, 256:TAPS], jnp.zeros((rows, TAPS_PAD - TAPS), BF16)], axis=1)
        shaped_ref[c, :, 256:TAPS_PAD] = tail


def build_hankel(extended_ref, hankel_ref, scale_ref, length, reach):
    sub = lax.broadcasted_iota(jnp.int32, (8, length), 0)
    for c in range(3):
        row = extended_ref[c : c + 1, :].astype(F32)
        stair = jnp.broadcast_to(row, (8, length))
        for bit in (1, 2, 4):
            stair = jnp.where((sub & bit) != 0, pltpu.roll(stair, length - bit, 1), stair)
        total = jnp.zeros((8, length), F32)
        square = jnp.zeros((8, length), F32)
        for m in range(0, 16, 2):
            pair = []
            for n in (m, m + 1):
                part = stair if n == 0 else pltpu.roll(stair, length - 8 * n, 1)
                pair.append(part)
                if n == 5:
                    early = jnp.where(sub < 4, part, 0.0)
                    tail_total, tail_square = total + early, square + early * early
                total = total + part
                square = square + part * part
            both = jnp.concatenate(pair, axis=0).astype(BF16)
            for j in range(3):
                hankel_ref[c, pl.ds(128 * j + 8 * m, 16), :] = both[:, 128 * j : 128 * j + reach]

        def window(whole, tail):
            whole = jnp.sum(whole, axis=0, keepdims=True)
            tail = jnp.sum(tail, axis=0, keepdims=True)
            return whole[:, 0:reach] + whole[:, 128 : 128 + reach] + tail[:, 256 : 256 + reach]

        mean = window(total, tail_total) / TAPS
        mean_square = window(square, tail_square) / TAPS
        scale_ref[c : c + 1, :] = 1.0 / (TAPS * jnp.sqrt(mean_square - mean * mean + 1e-06))


def correlate_kernel(blocks, out_len, extended_ref, moves_ref, *refs):
    shaped_refs = refs[:blocks]
    keep_ref, send_ref, hankel_ref, scale_ref = refs[blocks:]
    own = keep_ref.shape[1]
    per = shaped_refs[0].shape[1]
    length = extended_ref.shape[1]
    reach = hankel_ref.shape[2]
    s = lax.axis_index("sta")
    k = lax.axis_index("tm")
    build_hankel(extended_ref, hankel_ref, scale_ref, length, reach)
    lane = lax.broadcasted_iota(jnp.int32, (own, LANES), 1)
    for i in range(blocks):
        block = k ^ i
        combined = jnp.zeros((per, reach), F32)
        for c in range(3):
            raw = jnp.dot(shaped_refs[i][c], hankel_ref[c], preferred_element_type=F32)
            combined = combined + raw * scale_ref[c : c + 1, :]
        for a in range(per // own):
            group = block * (per // own) + a
            move = column_of(moves_ref[pl.ds(group, 1), :], own)
            low = move & (LANES - 1)
            spot = (lane + low) & (LANES - 1)
            inside = lane + low < LANES
            far = jnp.broadcast_to(move >= LANES, (own, LANES))
            part = combined[a * own : (a + 1) * own]
            turned = [
                jnp.take_along_axis(part[:, b * LANES : (b + 1) * LANES], spot, axis=1)
                for b in range(reach // LANES)
            ]
            near = [jnp.where(inside, turned[b], turned[b + 1]) for b in range(reach // LANES - 1)]
            index = (s ^ group) // 2
            result = jnp.concatenate(
                [jnp.where(far, near[b + 1], near[b]) for b in range(out_len // LANES)], axis=1
            )
            mine = (s ^ group) % 2 == 0

            @pl.when(mine)
            def _():
                keep_ref[index] = result

            @pl.when(jnp.logical_not(mine))
            def _():
                send_ref[index] = result


def exchange(block, axis, distance):
    return lax.ppermute(block, axis, [(i, i ^ distance) for i in range(lax.axis_size(axis))])


def per_device(records, templates, channel_mask, moveouts):
    records, templates, channel_mask = records[0], templates[0], channel_mask[0]
    stations, blocks = lax.axis_size("sta"), lax.axis_size("tm")
    slab = records.shape[1]
    per = templates.shape[1]
    own = per * blocks // stations
    following = lax.ppermute(records, "tm", [(i, i - 1) for i in range(1, blocks)])
    extended = jnp.concatenate([records, following], axis=1)
    moves = moveouts.reshape(stations, own)
    shaped = pl.pallas_call(
        shape_kernel,
        out_shape=jax.ShapeDtypeStruct((3, per, TAPS_PAD), BF16),
        name="shape_templates",
    )(templates, channel_mask)
    library = [shaped] + [exchange(shaped, "tm", d) for d in range(1, blocks)]
    reach = slab + 256
    half = jax.ShapeDtypeStruct((stations // 2, own, slab), F32)
    keep, send = pl.pallas_call(
        functools.partial(correlate_kernel, blocks, slab),
        out_shape=(half, half),
        scratch_shapes=[pltpu.VMEM((3, TAPS_PAD, reach), BF16), pltpu.VMEM((3, reach), F32)],
        name="correlate",
    )(extended, moves, *library)
    chips = keep + exchange(send, "sta", 1)
    arrived = [exchange(chips[d], "sta", 2 * d) for d in range(1, stations // 2)]
    stacked = chips[0]
    for part in arrived:
        stacked = stacked + part
    return stacked


def solution(mesh):
    return jax.shard_map(
        per_device,
        mesh=mesh,
        in_specs=(
            P("sta", None, "tm"),
            P("sta", None, "tm", None),
            P("sta", None, "tm"),
            P("sta", None),
        ),
        out_specs=P("sta", "tm"),
        check_vma=False,
    )
```

profile of v0, /device:TPU:0, one launch (start us, length us, event | category | flops | bytes accessed | tf_op | source)
XLA Modules:
  0.0 39.0 jit_solution(16626841404426004285)
XLA Ops:
  0.0 1.3 %copy.7 = s32[1,3,64]{2,1,0:T(4,128)} copy(s32[1,3,64]{2,0,1:T(1,128)} %param.6) | data formatting | bytes 1536
  1.3 0.0 copy-start.3
  1.3 1.8 %shape_templates.1.refs_0_ = bf16[3,64,384]{2,1,0:T(8,128)(2,1)} custom-call(bf16[3,64,300]{2,1,0:T(8,128)(2,1)} %bitcast.19, s32[3,64]{1,0:T(4,128)} %bitcast.20), custom_call_target="tpu_custom_call" | custom-call | tf_op jit(solution)/shard_map/shape_templates/pallas_call | solution.py:129
  3.1 5.0 %collective-permute-start.3 = (bf16[3,64,384]{2,1,0:T(8,128)(2,1)}, bf16[3,64,384]{2,1,0:T(8,128)(2,1)S(1)}, u32[]{:S(2)}, u32[]{:S(2)}) collective-permute-start(bf16[3,64,384]{2,1,0:T(8,128)(2,1)} %shape_templates.1.refs_0_), channel_id=1, source_target_pairs={{0,3},{1,2},{2,1},{3,0},{4,7},{5,6},{6,5},{7,4},{8,11},{9,10},{10,... | collective-permute-start | bytes 442376 | tf_op jit(solution)/shard_map/ppermute | solution.py:117
  8.1 0.0 collective-permute-start.2
  8.1 0.6 %collective-permute-start.1 = (bf16[3,64,384]{2,1,0:T(8,128)(2,1)}, bf16[3,64,384]{2,1,0:T(8,128)(2,1)S(1)}, u32[]{:S(2)}, u32[]{:S(2)}) collective-permute-start(bf16[3,64,384]{2,1,0:T(8,128)(2,1)} %shape_templates.1.refs_0_), channel_id=1, source_target_pairs={{0,1},{1,0},{2,3},{3,2},{4,5},{5,4},{6,7},{7,6},{8,9},{9,8},{10,11... | collective-permute-start | bytes 442376 | tf_op jit(solution)/shard_map/ppermute | solution.py:117
  8.7 0.0 copy-done.3
  8.7 0.0 copy-start.4
  8.7 1.4 %collective-permute-start = (bf16[3,512]{1,0:T(4,128)(2,1)S(1)}, bf16[3,512]{1,0:T(4,128)(2,1)S(1)}, u32[]{:S(2)}, u32[]{:S(2)}) collective-permute-start(bf16[3,512]{1,0:T(4,128)(2,1)S(1)} %bitcast.21), channel_id=1, source_target_pairs={{1,0},{2,1},{3,2},{5,4},{6,5},{7,6},{9,8},{10,9},{11,10},{13,12},{... | collective-permute-start | bytes 9224 | tf_op jit(solution)/shard_map/ppermute | solution.py:126
  10.1 0.5 %broadcast.3 = s32[]{:T(128)} broadcast(s32[]{:T(128)} %constant.12), dimensions={} | broadcast | bytes 8 | tf_op args[3]
  10.6 0.0 copy-done.4
  10.6 0.7 %reduce.3 = s32[256]{0:T(256)S(1)} reduce(s32[1,256]{1,0:T(1,128)S(1)} %copy-done.4, s32[]{:T(128)} %broadcast.3), dimensions={0}, to_apply=%param.7.reduce_sub_computation.3 | reduce | bytes 2052 | tf_op args[3]
  11.3 0.7 %reshape.3.moves_ref = s32[8,32]{1,0:T(8,128)} reshape(s32[256]{0:T(256)S(1)} %reduce.3) | data formatting | bytes 2048 | tf_op jit(solution)/shard_map/reshape | solution.py:128
  12.0 3.6 %collective-permute-done = bf16[3,512]{1,0:T(4,128)(2,1)S(1)} collective-permute-done((bf16[3,512]{1,0:T(4,128)(2,1)S(1)}, bf16[3,512]{1,0:T(4,128)(2,1)S(1)}, u32[]{:S(2)}, u32[]{:S(2)}) %collective-permute-start) | collective-permute-done | bytes 3104 | tf_op jit(solution)/shard_map/ppermute | solution.py:126
  15.5 0.6 %pad_maximum_fusion.extended_ref = bf16[3,1024]{1,0:T(4,128)(2,1)} fusion(bf16[3,512]{1,0:T(4,128)(2,1)S(1)} %collective-permute-done, bf16[3,512]{1,0:T(4,128)(2,1)S(1)} %bitcast.22), kind=kLoop, calls=%fused_computation.7 | loop fusion | flops 12288 | bytes 12288 | tf_op jit(solution)/shard_map/concatenate | solution.py:127
  16.1 0.0 collective-permute-done.3.refs_3_
  16.1 4.7 %collective-permute-done.2.refs_2_ = bf16[3,64,384]{2,1,0:T(8,128)(2,1)S(1)} collective-permute-done((bf16[3,64,384]{2,1,0:T(8,128)(2,1)}, bf16[3,64,384]{2,1,0:T(8,128)(2,1)S(1)}, u32[]{:S(2)}, u32[]{:S(2)}) %collective-permute-start.2) | collective-permute-done | bytes 147488 | tf_op jit(solution)/shard_map/ppermute | solution.py:117
  20.9 0.0 collective-permute-done.1.refs_1_
  20.9 0.0 copy-done
  20.9 0.6 %copy-done.1 = bf16[3,64,384]{2,1,0:T(8,128)(2,1)} copy-done((bf16[3,64,384]{2,1,0:T(8,128)(2,1)}, bf16[3,64,384]{2,1,0:T(8,128)(2,1)S(1)}, u32[]{:S(2)}) %copy-start.1) | copy-done | bytes 147480
  21.5 0.7 %copy-done.2 = bf16[3,64,384]{2,1,0:T(8,128)(2,1)} copy-done((bf16[3,64,384]{2,1,0:T(8,128)(2,1)}, bf16[3,64,384]{2,1,0:T(8,128)(2,1)S(1)}, u32[]{:S(2)}) %copy-start.2) | copy-done | bytes 147480
  22.2 5.6 %correlate.1 = (f32[4,32,512]{2,1,0:T(8,128)}, f32[4,32,512]{2,1,0:T(8,128)}) custom-call(bf16[3,1024]{1,0:T(4,128)(2,1)} %pad_maximum_fusion.extended_ref, s32[8,32]{1,0:T(8,128)} %reshape.3.moves_ref, bf16[3,64,384]{2,1,0:T(8,128)(2,1)} %shape_templates.1.refs_0_, bf16[3,64,384]{2,1,0:T(8,128)(2,1)} %copy-done.2, bf16[3,64,384]{2,1,0:T(8,128)(2,1)} %copy-done.1, ...), custom_call_target="tpu_custom_call" | custom-call | tf_op jit(solution)/shard_map/correlate/pallas_call | solution.py:137
  27.7 0.0 collective-permute-start.4
  27.7 1.7 %collective-permute-done.4 = f32[4,32,512]{2,1,0:T(8,128)S(1)} collective-permute-done((f32[4,32,512]{2,1,0:T(8,128)}, f32[4,32,512]{2,1,0:T(8,128)S(1)}, u32[]{:S(2)}, u32[]{:S(2)}) %collective-permute-start.4) | collective-permute-done | bytes 262176 | tf_op jit(solution)/shard_map/ppermute | solution.py:117
  29.5 1.0 %add.12 = f32[4,32,512]{2,1,0:T(8,128)S(1)} add(f32[4,32,512]{2,1,0:T(8,128)} %get-tuple-element.7, f32[4,32,512]{2,1,0:T(8,128)S(1)} %collective-permute-done.4) | non-fusion elementwise | flops 65536 | bytes 786432 | tf_op jit(solution)/shard_map/add | solution.py:143
  30.5 1.6 %collective-permute-start.5 = (f32[32,512]{1,0:T(8,128)S(1)}, f32[32,512]{1,0:T(8,128)S(1)}, u32[]{:S(2)}, u32[]{:S(2)}) collective-permute-start(f32[32,512]{1,0:T(8,128)S(1)} %get-tuple-element.9), channel_id=1, source_target_pairs={{0,8},{4,12},{8,0},{12,4},{16,24},{20,28},{24,16},{28,20},{1,9},{5... | collective-permute-start | bytes 196616 | tf_op jit(solution)/shard_map/ppermute | solution.py:117
  32.0 1.5 %collective-permute-start.7 = (f32[32,512]{1,0:T(8,128)S(1)}, f32[32,512]{1,0:T(8,128)S(1)}, u32[]{:S(2)}, u32[]{:S(2)}) collective-permute-start(f32[32,512]{1,0:T(8,128)S(1)} %get-tuple-element.10), channel_id=1, source_target_pairs={{0,24},{4,28},{8,16},{12,20},{16,8},{20,12},{24,0},{28,4},{1,25},{... | collective-permute-start | bytes 196616 | tf_op jit(solution)/shard_map/ppermute | solution.py:117
  33.5 0.5 %collective-permute-start.6 = (f32[32,512]{1,0:T(8,128)S(1)}, f32[32,512]{1,0:T(8,128)S(1)}, u32[]{:S(2)}, u32[]{:S(2)}) collective-permute-start(f32[32,512]{1,0:T(8,128)S(1)} %get-tuple-element.11), channel_id=1, source_target_pairs={{0,16},{4,20},{8,24},{12,28},{16,0},{20,4},{24,8},{28,12},{1,17},{... | collective-permute-start | bytes 196616 | tf_op jit(solution)/shard_map/ppermute | solution.py:117
  34.0 0.8 %collective-permute-done.5 = f32[32,512]{1,0:T(8,128)S(1)} collective-permute-done((f32[32,512]{1,0:T(8,128)S(1)}, f32[32,512]{1,0:T(8,128)S(1)}, u32[]{:S(2)}, u32[]{:S(2)}) %collective-permute-start.5) | collective-permute-done | bytes 65568 | tf_op jit(solution)/shard_map/ppermute | solution.py:117
  34.8 2.5 %collective-permute-done.7 = f32[32,512]{1,0:T(8,128)S(1)} collective-permute-done((f32[32,512]{1,0:T(8,128)S(1)}, f32[32,512]{1,0:T(8,128)S(1)}, u32[]{:S(2)}, u32[]{:S(2)}) %collective-permute-start.7) | collective-permute-done | bytes 65568 | tf_op jit(solution)/shard_map/ppermute | solution.py:117
  37.3 1.1 %collective-permute-done.6 = f32[32,512]{1,0:T(8,128)S(1)} collective-permute-done((f32[32,512]{1,0:T(8,128)S(1)}, f32[32,512]{1,0:T(8,128)S(1)}, u32[]{:S(2)}, u32[]{:S(2)}) %collective-permute-start.6) | collective-permute-done | bytes 65568 | tf_op jit(solution)/shard_map/ppermute | solution.py:117
  38.4 0.6 %fusion.2 = f32[32,512]{1,0:T(8,128)} fusion(f32[32,512]{1,0:T(8,128)S(1)} %collective-permute-done.7, f32[32,512]{1,0:T(8,128)S(1)} %collective-permute-done.6, f32[32,512]{1,0:T(8,128)S(1)} %collective-permute-done.5, f32[4,32,512]{2,1,0:T(8,128)S(1)} %add.12), kind=kLoop, calls=%fused_computation.6 | loop fusion | flops 49152 | bytes 327680 | tf_op jit(solution)/shard_map/add | solution.py:147
  (4 shorter events, 0.0 us)
Async XLA Ops:
  1.3 7.4 %copy-start.3 = (bf16[1,3,512]{2,1,0:T(4,128)(2,1)S(1)}, bf16[1,3,512]{2,1,0:T(4,128)(2,1)}, u32[]{:S(2)}) copy-start(bf16[1,3,512]{2,1,0:T(4,128)(2,1)} %param.4) | copy-start | bytes 9220
  3.1 13.1 %collective-permute-start.3 = (bf16[3,64,384]{2,1,0:T(8,128)(2,1)}, bf16[3,64,384]{2,1,0:T(8,128)(2,1)S(1)}, u32[]{:S(2)}, u32[]{:S(2)}) collective-permute-start(bf16[3,64,384]{2,1,0:T(8,128)(2,1)} %shape_templates.1.refs_0_), channel_id=1, source_target_pairs={{0,3},{1,2},{2,1},{3,0},{4,7},{5,6},{6,5},{7,4},{8,11},{9,10},{10,... | collective-permute-start | bytes 442376 | tf_op jit(solution)/shard_map/ppermute | solution.py:117
  8.1 12.7 %collective-permute-start.2 = (bf16[3,64,384]{2,1,0:T(8,128)(2,1)}, bf16[3,64,384]{2,1,0:T(8,128)(2,1)S(1)}, u32[]{:S(2)}, u32[]{:S(2)}) collective-permute-start(bf16[3,64,384]{2,1,0:T(8,128)(2,1)} %shape_templates.1.refs_0_), channel_id=1, source_target_pairs={{0,2},{1,3},{2,0},{3,1},{4,6},{5,7},{6,4},{7,5},{8,10},{9,11},{10,... | collective-permute-start | bytes 442376 | tf_op jit(solution)/shard_map/ppermute | solution.py:117
  8.1 12.7 %collective-permute-start.1 = (bf16[3,64,384]{2,1,0:T(8,128)(2,1)}, bf16[3,64,384]{2,1,0:T(8,128)(2,1)S(1)}, u32[]{:S(2)}, u32[]{:S(2)}) collective-permute-start(bf16[3,64,384]{2,1,0:T(8,128)(2,1)} %shape_templates.1.refs_0_), channel_id=1, source_target_pairs={{0,1},{1,0},{2,3},{3,2},{4,5},{5,4},{6,7},{7,6},{8,9},{9,8},{10,11... | collective-permute-start | bytes 442376 | tf_op jit(solution)/shard_map/ppermute | solution.py:117
  8.7 1.9 %copy-start.4 = (s32[1,256]{1,0:T(1,128)S(1)}, s32[1,256]{1,0:T(1,128)}, u32[]{:S(2)}) copy-start(s32[1,256]{1,0:T(1,128)} %param.7) | copy-start | bytes 3076
  8.7 6.8 %collective-permute-start = (bf16[3,512]{1,0:T(4,128)(2,1)S(1)}, bf16[3,512]{1,0:T(4,128)(2,1)S(1)}, u32[]{:S(2)}, u32[]{:S(2)}) collective-permute-start(bf16[3,512]{1,0:T(4,128)(2,1)S(1)} %bitcast.21), channel_id=1, source_target_pairs={{1,0},{2,1},{3,2},{5,4},{6,5},{7,6},{9,8},{10,9},{11,10},{13,12},{... | collective-permute-start | bytes 9224 | tf_op jit(solution)/shard_map/ppermute | solution.py:126
  16.1 4.7 %copy-start = (bf16[3,64,384]{2,1,0:T(8,128)(2,1)}, bf16[3,64,384]{2,1,0:T(8,128)(2,1)S(1)}, u32[]{:S(2)}) copy-start(bf16[3,64,384]{2,1,0:T(8,128)(2,1)S(1)} %collective-permute-done.3.refs_3_) | copy-start | bytes 442372
  20.9 0.6 %copy-start.1 = (bf16[3,64,384]{2,1,0:T(8,128)(2,1)}, bf16[3,64,384]{2,1,0:T(8,128)(2,1)S(1)}, u32[]{:S(2)}) copy-start(bf16[3,64,384]{2,1,0:T(8,128)(2,1)S(1)} %collective-permute-done.2.refs_2_) | copy-start | bytes 442372
  21.5 0.7 %copy-start.2 = (bf16[3,64,384]{2,1,0:T(8,128)(2,1)}, bf16[3,64,384]{2,1,0:T(8,128)(2,1)S(1)}, u32[]{:S(2)}) copy-start(bf16[3,64,384]{2,1,0:T(8,128)(2,1)S(1)} %collective-permute-done.1.refs_1_) | copy-start | bytes 442372
  27.7 1.7 %collective-permute-start.4 = (f32[4,32,512]{2,1,0:T(8,128)}, f32[4,32,512]{2,1,0:T(8,128)S(1)}, u32[]{:S(2)}, u32[]{:S(2)}) collective-permute-start(f32[4,32,512]{2,1,0:T(8,128)} %get-tuple-element.8), channel_id=1, source_target_pairs={{0,4},{4,0},{8,12},{12,8},{16,20},{20,16},{24,28},{28,24},{1,5},{5... | collective-permute-start | bytes 786440 | tf_op jit(solution)/shard_map/ppermute | solution.py:117
  30.5 4.3 %collective-permute-start.5 = (f32[32,512]{1,0:T(8,128)S(1)}, f32[32,512]{1,0:T(8,128)S(1)}, u32[]{:S(2)}, u32[]{:S(2)}) collective-permute-start(f32[32,512]{1,0:T(8,128)S(1)} %get-tuple-element.9), channel_id=1, source_target_pairs={{0,8},{4,12},{8,0},{12,4},{16,24},{20,28},{24,16},{28,20},{1,9},{5... | collective-permute-start | bytes 196616 | tf_op jit(solution)/shard_map/ppermute | solution.py:117
  32.0 5.2 %collective-permute-start.7 = (f32[32,512]{1,0:T(8,128)S(1)}, f32[32,512]{1,0:T(8,128)S(1)}, u32[]{:S(2)}, u32[]{:S(2)}) collective-permute-start(f32[32,512]{1,0:T(8,128)S(1)} %get-tuple-element.10), channel_id=1, source_target_pairs={{0,24},{4,28},{8,16},{12,20},{16,8},{20,12},{24,0},{28,4},{1,25},{... | collective-permute-start | bytes 196616 | tf_op jit(solution)/shard_map/ppermute | solution.py:117
  33.5 4.8 %collective-permute-start.6 = (f32[32,512]{1,0:T(8,128)S(1)}, f32[32,512]{1,0:T(8,128)S(1)}, u32[]{:S(2)}, u32[]{:S(2)}) collective-permute-start(f32[32,512]{1,0:T(8,128)S(1)} %get-tuple-element.11), channel_id=1, source_target_pairs={{0,16},{4,20},{8,24},{12,28},{16,0},{20,4},{24,8},{28,12},{1,17},{... | collective-permute-start | bytes 196616 | tf_op jit(solution)/shard_map/ppermute | solution.py:117
where the time goes:
time: 39.2 us; the launch traced here: 39 us
  waiting for transfers between devices  14.3 us (36%)
  starting transfers between devices  10.6 us (27%)
  Pallas kernels  7.37 us (19%)
  local copies, waits for them, and re-layouts  3.77 us (10%)
  other arithmetic  2.91 us (7%)
    ppermute x7, waiting for transfers between devices, exchange(): lax.ppermute(block, axis, [(i, i ^ distance) for i in range(lax.axis_size...  10.8 us
    ppermute x7, starting transfers between devices, exchange(): lax.ppermute(block, axis, [(i, i ^ distance) for i in range(lax.axis_size...  9.17 us
    pallas_call x1, Pallas kernels, per_device(): pl.pallas_call(functools.partial(correlate_kernel, blocks, slab), out_sha...  5.56 us
    ppermute x1, waiting for transfers between devices, per_device(): lax.ppermute(records, 'tm', [(i, i - 1) for i in range(1, blocks)])  3.56 us
    unnamed x12, local copies, waits for them, and re-layouts  3.08 us
    pallas_call x1, Pallas kernels, per_device(): pl.pallas_call(shape_kernel, out_shape=jax.ShapeDtypeStruct((3, per, TAPS...  1.81 us
    ppermute x1, starting transfers between devices, per_device(): lax.ppermute(records, 'tm', [(i, i - 1) for i in range(1, blocks)])  1.41 us
    add x1, other arithmetic, per_device(): chips = keep + exchange(send, 'sta', 1)  0.99 us
  transfers between devices with their start and end apart: 8, of which 6 were waited for; matrix products, arithmetic and copies ran while one was open for 6% of the time, Pallas kernels for 0%

commit v1 on v0

v1 whole, which is shorter than its diff:
```python
import functools
import jax
import jax.numpy as jnp
from jax import lax
from jax.experimental import pallas as pl
from jax.experimental.pallas import tpu as pltpu
from jax.sharding import PartitionSpec as P

TAPS = 300
TAPS_PAD = 384
LANES = 128
F32 = jnp.float32
BF16 = jnp.bfloat16
COST = {"correlate_own": 2 * 10**9, "correlate_middle": 2 * 10**9, "correlate_last": 5 * 10**8}
PARAMS = pltpu.CompilerParams(vmem_limit_bytes=16 << 20)


def column_of(row, rows, first):
    n = row.shape[1]
    wide = jnp.broadcast_to(row, (rows, n))
    here = lax.broadcasted_iota(jnp.int32, (rows, n), 0) + first
    at = here == lax.broadcasted_iota(jnp.int32, (rows, n), 1)
    return jnp.sum(jnp.where(at, wide, jnp.zeros_like(wide)), axis=1, keepdims=True)


def shape_kernel(
    templates_hbm, mask_hbm, slab_hbm, moves_hbm,
    shaped_ref, slab_ref, moves_ref,
    templates_ref, mask_ref, sems,
):
    pairs = (
        (templates_hbm, templates_ref), (mask_hbm, mask_ref), (slab_hbm, slab_ref), (moves_hbm, moves_ref)
    )
    copies = [pltpu.make_async_copy(a, b, sems.at[n]) for n, (a, b) in enumerate(pairs)]
    for copy in copies:
        copy.start()
    for copy in copies:
        copy.wait()
    per = templates_ref.shape[1]
    rows = 3 * per
    tails = []
    for c in range(3):
        values = templates_ref[c].astype(F32)
        center = jnp.sum(values, axis=1, keepdims=True) / TAPS
        spread = values - center
        rms = jnp.sqrt(jnp.sum(spread * spread, axis=1, keepdims=True) / TAPS + 1e-06)
        weight = column_of(mask_ref[c].astype(F32), per, 0)
        shaped = spread / rms * weight
        shaped_ref[c * per : (c + 1) * per, :] = shaped[:, 0:128].astype(BF16)
        shaped_ref[rows + c * per : rows + (c + 1) * per, :] = shaped[:, 128:256].astype(BF16)
        tails.append(jnp.concatenate([shaped[:, 256:TAPS], jnp.zeros((per, TAPS_PAD - TAPS), F32)], axis=1))
    tail = jnp.concatenate(tails, axis=0)
    shaped_ref[2 * rows :, :] = (tail[: rows // 2] + pltpu.roll(tail[rows // 2 :], 64, 1)).astype(BF16)


def unpack(shaped_ref, rows):
    packed = shaped_ref[2 * rows :, :].astype(F32)
    lane = lax.broadcasted_iota(jnp.int32, packed.shape, 1)
    low = jnp.where(lane < 64, packed, 0.0)
    high = jnp.where(lane < 64, pltpu.roll(packed, 64, 1), 0.0)
    tail = jnp.concatenate([low, high], axis=0).astype(BF16)
    return jnp.concatenate([shaped_ref[0:rows, :], shaped_ref[rows : 2 * rows, :], tail], axis=1)


def build_hankel(slab_ref, following_ref, hankel_ref, scale_ref):
    length = slab_ref.shape[1] + following_ref.shape[1]
    reach = hankel_ref.shape[2]
    sub = lax.broadcasted_iota(jnp.int32, (8, length), 0)
    for c in range(3):
        row = jnp.concatenate([slab_ref[c : c + 1, :], following_ref[c : c + 1, :]], axis=1).astype(F32)
        stair = jnp.broadcast_to(row, (8, length))
        for bit in (1, 2, 4):
            stair = jnp.where((sub & bit) != 0, pltpu.roll(stair, length - bit, 1), stair)
        total = jnp.zeros((8, length), F32)
        square = jnp.zeros((8, length), F32)
        for m in range(0, 16, 2):
            pair = []
            for n in (m, m + 1):
                part = stair if n == 0 else pltpu.roll(stair, length - 8 * n, 1)
                pair.append(part)
                if n == 5:
                    early = jnp.where(sub < 4, part, 0.0)
                    tail_total, tail_square = total + early, square + early * early
                total = total + part
                square = square + part * part
            both = jnp.concatenate(pair, axis=0).astype(BF16)
            for j in range(3):
                hankel_ref[c, pl.ds(128 * j + 8 * m, 16), :] = both[:, 128 * j : 128 * j + reach]

        def window(whole, tail):
            whole = jnp.sum(whole, axis=0, keepdims=True)
            tail = jnp.sum(tail, axis=0, keepdims=True)
            return whole[:, 0:reach] + whole[:, 128 : 128 + reach] + tail[:, 256 : 256 + reach]

        mean = window(total, tail_total) / TAPS
        mean_square = window(square, tail_square) / TAPS
        scale_ref[c : c + 1, :] = 1.0 / (TAPS * jnp.sqrt(mean_square - mean * mean + 1e-06))


def correlate(shaped, block, hankel_ref, scale_ref, moves_ref, out_len):
    per, reach = shaped.shape[0] // 3, hankel_ref.shape[2]
    combined = jnp.zeros((per, reach), F32)
    for c in range(3):
        raw = jnp.dot(shaped[c * per : (c + 1) * per], hankel_ref[c], preferred_element_type=F32)
        combined = combined + raw * scale_ref[c : c + 1, :]
    move = column_of(moves_ref[...].astype(F32), per, block * per).astype(jnp.int32)
    low = jnp.broadcast_to(move & (LANES - 1), (per, LANES))
    ahead = lax.broadcasted_iota(jnp.int32, (per, LANES), 1) + low
    spot = ahead & (LANES - 1)
    inside = ahead < LANES
    far = jnp.broadcast_to(move >= LANES, (per, LANES))
    turned = [
        jnp.take_along_axis(combined[:, b * LANES : (b + 1) * LANES], spot, axis=1)
        for b in range(reach // LANES)
    ]
    near = [jnp.where(inside, turned[b], turned[b + 1]) for b in range(reach // LANES - 1)]
    return jnp.concatenate([jnp.where(far, near[b + 1], near[b]) for b in range(out_len // LANES)], axis=1)


def store_halves(result, keep_ref, send_ref, spot):
    own = keep_ref.shape[1]
    odd = lax.axis_index("sta") % 2 == 1
    keep_ref[spot] = jnp.where(odd, result[own:], result[:own])
    send_ref[spot] = jnp.where(odd, result[:own], result[own:])


def first_kernel(slab_ref, following_ref, moves_ref, shaped_ref, hankel_ref, scale_ref, keep_ref, send_ref):
    build_hankel(slab_ref, following_ref, hankel_ref, scale_ref)
    shaped = unpack(shaped_ref, 6 * keep_ref.shape[1])
    result = correlate(shaped, lax.axis_index("tm"), hankel_ref, scale_ref, moves_ref, keep_ref.shape[2])
    store_halves(result, keep_ref, send_ref, 0)


def middle_kernel(blocks, hankel_ref, scale_ref, moves_ref, early_keep_ref, early_send_ref, *refs):
    keep_ref, send_ref = refs[blocks:]
    keep_ref[0] = early_keep_ref[0]
    send_ref[0] = early_send_ref[0]
    for i in range(blocks):
        shaped = unpack(refs[i], 6 * keep_ref.shape[1])
        block = lax.axis_index("tm") ^ (i + 1)
        result = correlate(shaped, block, hankel_ref, scale_ref, moves_ref, keep_ref.shape[2])
        store_halves(result, keep_ref, send_ref, i + 1)


def last_kernel(distance, hankel_ref, scale_ref, moves_ref, shaped_ref, keep_ref, send_ref):
    shaped = unpack(shaped_ref, 6 * keep_ref.shape[1])
    block = lax.axis_index("tm") ^ distance
    result = correlate(shaped, block, hankel_ref, scale_ref, moves_ref, keep_ref.shape[2])
    store_halves(result, keep_ref, send_ref, 0)


def assemble_kernel(keep_ref, arrived_ref, last_keep_ref, last_arrived_ref, *out_refs):
    chip = lax.axis_index("sta") // 2
    blocks = keep_ref.shape[0] + 1
    for i in range(blocks):
        target = chip ^ lax.axis_index("tm") ^ i
        if i < blocks - 1:
            value = keep_ref[i] + arrived_ref[i]
        else:
            value = last_keep_ref[0] + last_arrived_ref[0]
        for j, out_ref in enumerate(out_refs):

            @pl.when(target == j)
            def _():
                out_ref[...] = value


def exchange(block, axis, distance):
    return lax.ppermute(block, axis, [(i, i ^ distance) for i in range(lax.axis_size(axis))])


def per_device(records, templates, channel_mask, moveouts):
    stations, blocks = lax.axis_size("sta"), lax.axis_size("tm")
    assert stations == 2 * blocks and records.shape[0] == 1
    slab = records.shape[2]
    per = templates.shape[2]
    own = per // 2
    rows = 3 * per

    def call(kernel, name, *shapes):
        cost = pl.CostEstimate(flops=COST.get(name, 10**6), bytes_accessed=0, transcendentals=0)
        return pl.pallas_call(kernel, out_shape=shapes, name=name, compiler_params=PARAMS, cost_estimate=cost)

    def terms(n):
        return jax.ShapeDtypeStruct((n, own, slab), F32)

    masks = channel_mask.transpose(1, 0, 2)
    shaped, slab_data, moves = pl.pallas_call(
        shape_kernel,
        out_shape=(
            jax.ShapeDtypeStruct((2 * rows + rows // 2, LANES), BF16),
            jax.ShapeDtypeStruct(records.shape[1:], BF16),
            jax.ShapeDtypeStruct(moveouts.shape, jnp.int32),
        ),
        in_specs=[pl.BlockSpec(memory_space=pltpu.HBM)] * 4,
        scratch_shapes=[
            pltpu.VMEM(templates.shape[1:], BF16),
            pltpu.VMEM(masks.shape, jnp.int32),
            pltpu.SemaphoreType.DMA((4,)),
        ],
        name="shape_templates",
        compiler_params=pltpu.CompilerParams(vmem_limit_bytes=60 << 20),
    )(templates[0], masks, records[0], moveouts)
    library = {i: exchange(shaped, "tm", i) for i in range(1, blocks)}
    following = lax.ppermute(slab_data, "tm", [(i, i - 1) for i in range(1, blocks)])
    hankel, scale, keep, send = call(
        first_kernel,
        "correlate_own",
        jax.ShapeDtypeStruct((3, TAPS_PAD, slab + 2 * LANES), BF16),
        jax.ShapeDtypeStruct((3, slab + 2 * LANES), F32),
        terms(1),
        terms(1),
    )(slab_data, following, moves, shaped)
    middle = [library[i] for i in range(1, blocks - 1)]
    keep, send = call(
        functools.partial(middle_kernel, blocks - 2), "correlate_middle", terms(blocks - 1), terms(blocks - 1)
    )(hankel, scale, moves, keep, send, *middle)
    arrived = exchange(send, "sta", 1)
    last_keep, last_send = call(
        functools.partial(last_kernel, blocks - 1), "correlate_last", terms(1), terms(1)
    )(hankel, scale, moves, library[blocks - 1])
    last_arrived = exchange(last_send, "sta", 1)
    piece = jax.ShapeDtypeStruct((own, slab), F32)
    chips = call(assemble_kernel, "add_cores", *[piece] * blocks)(keep, arrived, last_keep, last_arrived)
    others = [exchange(chips[d], "sta", 2 * d) for d in range(1, blocks)]
    stacked = chips[0]
    for part in others:
        stacked = stacked + part
    return stacked


def solution(mesh):
    return jax.shard_map(
        per_device,
        mesh=mesh,
        in_specs=(
            P("sta", None, "tm"),
            P("sta", None, "tm", None),
            P("sta", None, "tm"),
            P("sta", None),
        ),
        out_specs=P("sta", "tm"),
        check_vma=False,
    )
```

time: 39.2 us -> 30.8 us (0.79)
  waiting for transfers between devices: 14.3 us -> 10.9 us
  Pallas kernels: 7.37 us -> 4.47 us
  other arithmetic: 2.91 us -> 0.65 us
  starting transfers between devices: 10.6 us -> 12.2 us
  local copies, waits for them, and re-layouts: 3.77 us -> 2.22 us
    ppermute x1, waiting for transfers between devices: 3.56 us -> 0.01 us  [per_device(): lax.ppermute(slab_data, 'tm', [(i, i - 1) for i in range(1, blocks)])]
    pallas_call x2 -> x5, Pallas kernels: 7.37 us -> 4.47 us  [the longest x1 1.88 us: per_device(): pl.pallas_call(shape_kernel, out_shape=(jax.ShapeDtypeStruct((2 * rows +...]
    ppermute x7 -> x8, starting transfers between devices: 9.17 us -> 10.9 us  [exchange(): lax.ppermute(block, axis, [(i, i ^ distance) for i in range(lax.axis_size...]
    add x1 -> x0, other arithmetic: 0.99 us -> none  [per_device(): chips = keep + exchange(send, 'sta', 1)]
    unnamed x12 -> x6, local copies, waits for them, and re-layouts: 3.08 us -> 2.22 us
    reshape x1 -> x0, local copies, waits for them, and re-layouts: 0.67 us -> none  [per_device(): moves = moveouts.reshape(stations, own)]
    unnamed x1 -> x0, other arithmetic: 0.66 us -> none
    concatenate x1 -> x0, other arithmetic: 0.6 us -> none  [per_device(): extended = jnp.concatenate([records, following], axis=1)]
  transfers between devices with their start and end apart: 8 -> 9, of which waited for: 6 -> 5; matrix products, arithmetic and copies ran while one was open for 6% -> 0% of each run, Pallas kernels for 0% -> 8%
where the time goes in v1:
time: 30.8 us; the launch traced here: 30.6 us
  starting transfers between devices  12.2 us (40%)
  waiting for transfers between devices  10.9 us (35%)
  Pallas kernels  4.47 us (15%)
  local copies, waits for them, and re-layouts  2.22 us (7%)
  other arithmetic  0.65 us (2%)
    ppermute x8, waiting for transfers between devices, exchange(): lax.ppermute(block, axis, [(i, i ^ distance) for i in range(lax.axis_size...  10.9 us
    ppermute x8, starting transfers between devices, exchange(): lax.ppermute(block, axis, [(i, i ^ distance) for i in range(lax.axis_size...  10.9 us
    unnamed x6, local copies, waits for them, and re-layouts  2.22 us
    pallas_call x1, Pallas kernels, per_device(): pl.pallas_call(shape_kernel, out_shape=(jax.ShapeDtypeStruct((2 * rows +...  1.88 us
    ppermute x1, starting transfers between devices, per_device(): lax.ppermute(slab_data, 'tm', [(i, i - 1) for i in range(1, blocks)])  1.29 us
    pallas_call x1, Pallas kernels, per_device(): call(first_kernel, 'correlate_own', jax.ShapeDtypeStruct((3, TAPS_PAD, sl...  1.14 us
    pallas_call x1, Pallas kernels, per_device(): call(functools.partial(middle_kernel, blocks - 2), 'correlate_middle', te...  0.87 us
    add x1, other arithmetic, per_device(): stacked = stacked + part  0.65 us
  transfers between devices with their start and end apart: 9, of which 5 were waited for; matrix products, arithmetic and copies ran while one was open for 0% of the time, Pallas kernels for 8%

profile of v1, /device:TPU:0, one launch (start us, length us, event | category | flops | bytes accessed | tf_op | source)
XLA Modules:
  0.0 30.6 jit_solution(10794094324118838283)
XLA Ops:
  0.0 1.9 %shape_templates.1 = (bf16[480,128]{1,0:T(8,128)(2,1)}, bf16[3,512]{1,0:T(4,128)(2,1)}, s32[1,256]{1,0:T(1,128)}) custom-call(bf16[3,64,300]{2,1,0:T(8,128)(2,1)} %bitcast.3, s32[3,1,64]{2,1,0:T(1,128)} %bitcast.5, bf16[3,512]{1,0:T(4,128)(2,1)} %bitcast.4, s32[1,256]{1,0:T(1,128)} %moves_hbm.1), custom_call_target="tpu_custom_call" | custom-call | tf_op jit(solution)/shard_map/shape_templates/pallas_call | solution.py:188
  1.9 1.3 %collective-permute-start = (bf16[3,512]{1,0:T(4,128)(2,1)}, bf16[3,512]{1,0:T(4,128)(2,1)S(1)}, u32[]{:S(2)}, u32[]{:S(2)}) collective-permute-start(bf16[3,512]{1,0:T(4,128)(2,1)} %get-tuple-element.20.slab_ref), channel_id=1, source_target_pairs={{1,0},{2,1},{3,2},{5,4},{6,5},{7,6},{9,8},{10,9},{11,10},{13,12},{... | collective-permute-start | bytes 9224 | tf_op jit(solution)/shard_map/ppermute | solution.py:205
  3.2 3.7 %collective-permute-start.1 = (bf16[480,128]{1,0:T(8,128)(2,1)}, bf16[480,128]{1,0:T(8,128)(2,1)S(1)}, u32[]{:S(2)}, u32[]{:S(2)}) collective-permute-start(bf16[480,128]{1,0:T(8,128)(2,1)} %get-tuple-element.22.shaped_ref), channel_id=1, source_target_pairs={{0,1},{1,0},{2,3},{3,2},{4,5},{5,4},{6,7},{7,6},{8,9},{9,8},{10,11... | collective-permute-start | bytes 368648 | tf_op jit(solution)/shard_map/ppermute | solution.py:169
  6.9 3.0 %collective-permute-start.2 = (bf16[480,128]{1,0:T(8,128)(2,1)}, bf16[480,128]{1,0:T(8,128)(2,1)S(1)}, u32[]{:S(2)}, u32[]{:S(2)}) collective-permute-start(bf16[480,128]{1,0:T(8,128)(2,1)} %get-tuple-element.22.shaped_ref), channel_id=1, source_target_pairs={{0,2},{1,3},{2,0},{3,1},{4,6},{5,7},{6,4},{7,5},{8,10},{9,11},{10,... | collective-permute-start | bytes 368648 | tf_op jit(solution)/shard_map/ppermute | solution.py:169
  9.9 0.0 collective-permute-start.4
  9.9 0.0 collective-permute-done.following_ref
  9.9 0.0 copy-start
  9.9 0.6 %copy-done = s32[1,256]{1,0:T(1,128)S(1)} copy-done((s32[1,256]{1,0:T(1,128)S(1)}, s32[1,256]{1,0:T(1,128)}, u32[]{:S(2)}) %copy-start) | copy-done | bytes 1048
  10.6 0.0 copy-start.1
  10.6 0.9 %copy-done.1 = bf16[480,128]{1,0:T(8,128)(2,1)S(1)} copy-done((bf16[480,128]{1,0:T(8,128)(2,1)S(1)}, bf16[480,128]{1,0:T(8,128)(2,1)}, u32[]{:S(2)}) %copy-start.1) | copy-done | bytes 122904
  11.5 0.0 copy-start.2
  11.5 0.7 %copy-done.2 = bf16[3,512]{1,0:T(4,128)(2,1)S(1)} copy-done((bf16[3,512]{1,0:T(4,128)(2,1)S(1)}, bf16[3,512]{1,0:T(4,128)(2,1)}, u32[]{:S(2)}) %copy-start.2) | copy-done | bytes 3096
  12.2 1.1 %correlate_own.1 = (bf16[3,384,768]{2,1,0:T(8,128)(2,1)S(1)}, f32[3,768]{1,0:T(4,128)S(1)}, f32[1,32,512]{2,1,0:T(8,128)S(1)}, f32[1,32,512]{2,1,0:T(8,128)S(1)}) custom-call(bf16[3,512]{1,0:T(4,128)(2,1)S(1)} %copy-done.2, bf16[3,512]{1,0:T(4,128)(2,1)S(1)} %collective-permute-done.following_ref, s32[1,256]{1,0:T(1,128)S(1)} %copy-done, ...), custom_call_target="tpu_custom_call" | custom-call | flops 2000000000 | tf_op jit(solution)/shard_map/correlate_own/pallas_call | solution.py:206
  13.3 0.0 collective-permute-done.1.refs_0_
  13.3 6.2 %collective-permute-done.2.refs_1_ = bf16[480,128]{1,0:T(8,128)(2,1)S(1)} collective-permute-done((bf16[480,128]{1,0:T(8,128)(2,1)}, bf16[480,128]{1,0:T(8,128)(2,1)S(1)}, u32[]{:S(2)}, u32[]{:S(2)}) %collective-permute-start.2) | collective-permute-done | bytes 122912 | tf_op jit(solution)/shard_map/ppermute | solution.py:169
  19.6 0.9 %correlate_middle.1 = (f32[3,32,512]{2,1,0:T(8,128)S(1)}, f32[3,32,512]{2,1,0:T(8,128)S(1)}) custom-call(bf16[3,384,768]{2,1,0:T(8,128)(2,1)S(1)} %get-tuple-element.23.hankel_ref, f32[3,768]{1,0:T(4,128)S(1)} %get-tuple-element.24.scale_ref, s32[1,256]{1,0:T(1,128)S(1)} %copy-done, f32[1,32,512]{2,1,0:T(8,128)S(1)} %get-tuple-element.25.early_keep_ref, ...), custom_call_target="tpu_custom_call" | custom-call | flops 2000000000 | tf_op jit(solution)/shard_map/correlate_middle/pallas_call | solution.py:215
  20.4 0.1 collective-permute-start.3
  20.5 0.0 collective-permute-done.4.shaped_ref
  20.5 0.5 %correlate_last.1 = (f32[1,32,512]{2,1,0:T(8,128)S(1)}, f32[1,32,512]{2,1,0:T(8,128)S(1)}) custom-call(bf16[3,384,768]{2,1,0:T(8,128)(2,1)S(1)} %get-tuple-element.23.hankel_ref, f32[3,768]{1,0:T(4,128)S(1)} %get-tuple-element.24.scale_ref, s32[1,256]{1,0:T(1,128)S(1)} %copy-done, bf16[480,128]{1,0:T(8,128)(2,1)S(1)} %collective-permute-done.4.shaped_ref), custom_call_target="tpu_custom_call" | custom-call | flops 500000000 | tf_op jit(solution)/shard_map/correlate_last/pallas_call | solution.py:219
  21.0 0.6 %collective-permute-start.5 = (f32[1,32,512]{2,1,0:T(8,128)S(1)}, f32[1,32,512]{2,1,0:T(8,128)S(1)}, u32[]{:S(2)}, u32[]{:S(2)}) collective-permute-start(f32[1,32,512]{2,1,0:T(8,128)S(1)} %get-tuple-element.30), channel_id=1, source_target_pairs={{0,4},{4,0},{8,12},{12,8},{16,20},{20,16},{24,28},{28,24},{1,5},{5... | collective-permute-start | bytes 196616 | tf_op jit(solution)/shard_map/ppermute | solution.py:169
  21.6 0.9 %collective-permute-done.5.last_arrived_ref = f32[1,32,512]{2,1,0:T(8,128)S(1)} collective-permute-done((f32[1,32,512]{2,1,0:T(8,128)S(1)}, f32[1,32,512]{2,1,0:T(8,128)S(1)}, u32[]{:S(2)}, u32[]{:S(2)}) %collective-permute-start.5) | collective-permute-done | bytes 65568 | tf_op jit(solution)/shard_map/ppermute | solution.py:169
  22.5 0.0 collective-permute-done.3.arrived_ref
  22.5 0.1 add_cores.1
  22.6 2.6 %collective-permute-start.8 = (f32[32,512]{1,0:T(8,128)S(1)}, f32[32,512]{1,0:T(8,128)S(1)}, u32[]{:S(2)}, u32[]{:S(2)}) collective-permute-start(f32[32,512]{1,0:T(8,128)S(1)} %get-tuple-element.34), channel_id=1, source_target_pairs={{0,24},{4,28},{8,16},{12,20},{16,8},{20,12},{24,0},{28,4},{1,25},{... | collective-permute-start | bytes 196616 | tf_op jit(solution)/shard_map/ppermute | solution.py:169
  25.1 0.5 %collective-permute-start.7 = (f32[32,512]{1,0:T(8,128)S(1)}, f32[32,512]{1,0:T(8,128)S(1)}, u32[]{:S(2)}, u32[]{:S(2)}) collective-permute-start(f32[32,512]{1,0:T(8,128)S(1)} %get-tuple-element.33), channel_id=1, source_target_pairs={{0,16},{4,20},{8,24},{12,28},{16,0},{20,4},{24,8},{28,12},{1,17},{... | collective-permute-start | bytes 196616 | tf_op jit(solution)/shard_map/ppermute | solution.py:169
  25.7 0.5 %collective-permute-start.6 = (f32[32,512]{1,0:T(8,128)S(1)}, f32[32,512]{1,0:T(8,128)S(1)}, u32[]{:S(2)}, u32[]{:S(2)}) collective-permute-start(f32[32,512]{1,0:T(8,128)S(1)} %get-tuple-element.32), channel_id=1, source_target_pairs={{0,8},{4,12},{8,0},{12,4},{16,24},{20,28},{24,16},{28,20},{1,9},{5... | collective-permute-start | bytes 196616 | tf_op jit(solution)/shard_map/ppermute | solution.py:169
  26.1 1.8 %collective-permute-done.8 = f32[32,512]{1,0:T(8,128)S(1)} collective-permute-done((f32[32,512]{1,0:T(8,128)S(1)}, f32[32,512]{1,0:T(8,128)S(1)}, u32[]{:S(2)}, u32[]{:S(2)}) %collective-permute-start.8) | collective-permute-done | bytes 65568 | tf_op jit(solution)/shard_map/ppermute | solution.py:169
  27.9 1.5 %collective-permute-done.7 = f32[32,512]{1,0:T(8,128)S(1)} collective-permute-done((f32[32,512]{1,0:T(8,128)S(1)}, f32[32,512]{1,0:T(8,128)S(1)}, u32[]{:S(2)}, u32[]{:S(2)}) %collective-permute-start.7) | collective-permute-done | bytes 65568 | tf_op jit(solution)/shard_map/ppermute | solution.py:169
  29.4 0.5 %collective-permute-done.6 = f32[32,512]{1,0:T(8,128)S(1)} collective-permute-done((f32[32,512]{1,0:T(8,128)S(1)}, f32[32,512]{1,0:T(8,128)S(1)}, u32[]{:S(2)}, u32[]{:S(2)}) %collective-permute-start.6) | collective-permute-done | bytes 65568 | tf_op jit(solution)/shard_map/ppermute | solution.py:169
  29.9 0.6 %add_add_fusion = f32[32,512]{1,0:T(8,128)} fusion(f32[32,512]{1,0:T(8,128)S(1)} %collective-permute-done.8, f32[32,512]{1,0:T(8,128)S(1)} %collective-permute-done.7, f32[32,512]{1,0:T(8,128)S(1)} %get-tuple-element.31, f32[32,512]{1,0:T(8,128)S(1)} %collective-permute-done.6), kind=kLoop, calls=%fused_computation | loop fusion | flops 49152 | bytes 327680 | tf_op jit(solution)/shard_map/add | solution.py:228
Async XLA Ops:
  1.9 8.0 %collective-permute-start = (bf16[3,512]{1,0:T(4,128)(2,1)}, bf16[3,512]{1,0:T(4,128)(2,1)S(1)}, u32[]{:S(2)}, u32[]{:S(2)}) collective-permute-start(bf16[3,512]{1,0:T(4,128)(2,1)} %get-tuple-element.20.slab_ref), channel_id=1, source_target_pairs={{1,0},{2,1},{3,2},{5,4},{6,5},{7,6},{9,8},{10,9},{11,10},{13,12},{... | collective-permute-start | bytes 9224 | tf_op jit(solution)/shard_map/ppermute | solution.py:205
  3.2 10.1 %collective-permute-start.1 = (bf16[480,128]{1,0:T(8,128)(2,1)}, bf16[480,128]{1,0:T(8,128)(2,1)S(1)}, u32[]{:S(2)}, u32[]{:S(2)}) collective-permute-start(bf16[480,128]{1,0:T(8,128)(2,1)} %get-tuple-element.22.shaped_ref), channel_id=1, source_target_pairs={{0,1},{1,0},{2,3},{3,2},{4,5},{5,4},{6,7},{7,6},{8,9},{9,8},{10,11... | collective-permute-start | bytes 368648 | tf_op jit(solution)/shard_map/ppermute | solution.py:169
  6.9 12.7 %collective-permute-start.2 = (bf16[480,128]{1,0:T(8,128)(2,1)}, bf16[480,128]{1,0:T(8,128)(2,1)S(1)}, u32[]{:S(2)}, u32[]{:S(2)}) collective-permute-start(bf16[480,128]{1,0:T(8,128)(2,1)} %get-tuple-element.22.shaped_ref), channel_id=1, source_target_pairs={{0,2},{1,3},{2,0},{3,1},{4,6},{5,7},{6,4},{7,5},{8,10},{9,11},{10,... | collective-permute-start | bytes 368648 | tf_op jit(solution)/shard_map/ppermute | solution.py:169
  9.9 10.6 %collective-permute-start.4 = (bf16[480,128]{1,0:T(8,128)(2,1)}, bf16[480,128]{1,0:T(8,128)(2,1)S(1)}, u32[]{:S(2)}, u32[]{:S(2)}) collective-permute-start(bf16[480,128]{1,0:T(8,128)(2,1)} %get-tuple-element.22.shaped_ref), channel_id=1, source_target_pairs={{0,3},{1,2},{2,1},{3,0},{4,7},{5,6},{6,5},{7,4},{8,11},{9,10},{10,... | collective-permute-start | bytes 368648 | tf_op jit(solution)/shard_map/ppermute | solution.py:169
  9.9 0.6 %copy-start = (s32[1,256]{1,0:T(1,128)S(1)}, s32[1,256]{1,0:T(1,128)}, u32[]{:S(2)}) copy-start(s32[1,256]{1,0:T(1,128)} %get-tuple-element.21.moves_ref) | copy-start | bytes 3076
  10.6 0.9 %copy-start.1 = (bf16[480,128]{1,0:T(8,128)(2,1)S(1)}, bf16[480,128]{1,0:T(8,128)(2,1)}, u32[]{:S(2)}) copy-start(bf16[480,128]{1,0:T(8,128)(2,1)} %get-tuple-element.22.shaped_ref) | copy-start | bytes 368644
  11.5 0.7 %copy-start.2 = (bf16[3,512]{1,0:T(4,128)(2,1)S(1)}, bf16[3,512]{1,0:T(4,128)(2,1)}, u32[]{:S(2)}) copy-start(bf16[3,512]{1,0:T(4,128)(2,1)} %get-tuple-element.20.slab_ref) | copy-start | bytes 9220
  20.4 2.1 %collective-permute-start.3 = (f32[3,32,512]{2,1,0:T(8,128)S(1)}, f32[3,32,512]{2,1,0:T(8,128)S(1)}, u32[]{:S(2)}, u32[]{:S(2)}) collective-permute-start(f32[3,32,512]{2,1,0:T(8,128)S(1)} %get-tuple-element.28), channel_id=1, source_target_pairs={{0,4},{4,0},{8,12},{12,8},{16,20},{20,16},{24,28},{28,24},{1,5},{5... | collective-permute-start | bytes 589832 | tf_op jit(solution)/shard_map/ppermute | solution.py:169
  21.0 1.5 %collective-permute-start.5 = (f32[1,32,512]{2,1,0:T(8,128)S(1)}, f32[1,32,512]{2,1,0:T(8,128)S(1)}, u32[]{:S(2)}, u32[]{:S(2)}) collective-permute-start(f32[1,32,512]{2,1,0:T(8,128)S(1)} %get-tuple-element.30), channel_id=1, source_target_pairs={{0,4},{4,0},{8,12},{12,8},{16,20},{20,16},{24,28},{28,24},{1,5},{5... | collective-permute-start | bytes 196616 | tf_op jit(solution)/shard_map/ppermute | solution.py:169
  22.6 5.3 %collective-permute-start.8 = (f32[32,512]{1,0:T(8,128)S(1)}, f32[32,512]{1,0:T(8,128)S(1)}, u32[]{:S(2)}, u32[]{:S(2)}) collective-permute-start(f32[32,512]{1,0:T(8,128)S(1)} %get-tuple-element.34), channel_id=1, source_target_pairs={{0,24},{4,28},{8,16},{12,20},{16,8},{20,12},{24,0},{28,4},{1,25},{... | collective-permute-start | bytes 196616 | tf_op jit(solution)/shard_map/ppermute | solution.py:169
  25.1 4.3 %collective-permute-start.7 = (f32[32,512]{1,0:T(8,128)S(1)}, f32[32,512]{1,0:T(8,128)S(1)}, u32[]{:S(2)}, u32[]{:S(2)}) collective-permute-start(f32[32,512]{1,0:T(8,128)S(1)} %get-tuple-element.33), channel_id=1, source_target_pairs={{0,16},{4,20},{8,24},{12,28},{16,0},{20,4},{24,8},{28,12},{1,17},{... | collective-permute-start | bytes 196616 | tf_op jit(solution)/shard_map/ppermute | solution.py:169
  25.7 4.3 %collective-permute-start.6 = (f32[32,512]{1,0:T(8,128)S(1)}, f32[32,512]{1,0:T(8,128)S(1)}, u32[]{:S(2)}, u32[]{:S(2)}) collective-permute-start(f32[32,512]{1,0:T(8,128)S(1)} %get-tuple-element.32), channel_id=1, source_target_pairs={{0,8},{4,12},{8,0},{12,4},{16,24},{20,28},{24,16},{28,20},{1,9},{5... | collective-permute-start | bytes 196616 | tf_op jit(solution)/shard_map/ppermute | solution.py:169

commit v2 on v1

v2 whole, which is shorter than its diff:
```python
import functools
import jax
import jax.numpy as jnp
from jax import lax
from jax.experimental import pallas as pl
from jax.experimental.pallas import tpu as pltpu
from jax.sharding import PartitionSpec as P

TAPS = 300
TAPS_PAD = 384
LANES = 128
F32 = jnp.float32
BF16 = jnp.bfloat16
SMALL = pltpu.CompilerParams(vmem_limit_bytes=16 << 20)
WIDE = pltpu.CompilerParams(vmem_limit_bytes=60 << 20)


def column_of(row, rows, first):
    n = row.shape[1]
    wide = jnp.broadcast_to(row, (rows, n))
    here = lax.broadcasted_iota(jnp.int32, (rows, n), 0) + first
    at = here == lax.broadcasted_iota(jnp.int32, (rows, n), 1)
    return jnp.sum(jnp.where(at, wide, jnp.zeros_like(wide)), axis=1, keepdims=True)


def shape_kernel(templates_hbm, mask_hbm, packed_ref, templates_ref, mask_ref, sems):
    per = templates_ref.shape[1]
    each = packed_ref.shape[0] // 3
    copies = [
        pltpu.make_async_copy(mask_hbm, mask_ref, sems.at[0]),
        pltpu.make_async_copy(templates_hbm, templates_ref, sems.at[1]),
    ]
    for copy in copies:
        copy.start()
    for copy in copies:
        copy.wait()
    for c in range(3):
        values = templates_ref[c].astype(F32)
        center = jnp.sum(values, axis=1, keepdims=True) / TAPS
        spread = values - center
        rms = jnp.sqrt(jnp.sum(spread * spread, axis=1, keepdims=True) / TAPS + 1e-06)
        weight = column_of(mask_ref[c].astype(F32), per, 0)
        shaped = spread / rms * weight
        tail = jnp.concatenate([shaped[:, 256:TAPS], jnp.zeros((per, TAPS_PAD - TAPS), F32)], axis=1)
        tail = tail[: per // 2] + pltpu.roll(tail[per // 2 :], 64, 1)
        rows = jnp.concatenate([shaped[:, 0:128], shaped[:, 128:256], tail], axis=0)
        packed_ref[c * each : (c + 1) * each] = rows.astype(BF16)


def unpack(rows):
    per = rows.shape[0] * 2 // 5
    packed = rows[2 * per :].astype(F32)
    lane = lax.broadcasted_iota(jnp.int32, packed.shape, 1)
    low = jnp.where(lane < 64, packed, 0.0)
    high = jnp.where(lane < 64, pltpu.roll(packed, 64, 1), 0.0)
    tail = jnp.concatenate([low, high], axis=0).astype(BF16)
    return jnp.concatenate([rows[0:per], rows[per : 2 * per], tail], axis=1)


def build_hankel(slab_ref, following_ref, hankel_ref, scale_ref):
    length = slab_ref.shape[1] + following_ref.shape[1]
    reach = hankel_ref.shape[2]
    sub = lax.broadcasted_iota(jnp.int32, (8, length), 0)
    for c in range(3):
        row = jnp.concatenate([slab_ref[c : c + 1, :], following_ref[c : c + 1, :]], axis=1).astype(F32)
        stair = jnp.broadcast_to(row, (8, length))
        for bit in (1, 2, 4):
            stair = jnp.where((sub & bit) != 0, pltpu.roll(stair, length - bit, 1), stair)
        total = jnp.zeros((8, length), F32)
        square = jnp.zeros((8, length), F32)
        for m in range(0, 16, 2):
            pair = []
            for n in (m, m + 1):
                part = stair if n == 0 else pltpu.roll(stair, length - 8 * n, 1)
                pair.append(part)
                if n == 5:
                    early = jnp.where(sub < 4, part, 0.0)
                    tail_total, tail_square = total + early, square + early * early
                total = total + part
                square = square + part * part
            both = jnp.concatenate(pair, axis=0).astype(BF16)
            for j in range(3):
                hankel_ref[c, pl.ds(128 * j + 8 * m, 16), :] = both[:, 128 * j : 128 * j + reach]

        def window(whole, tail):
            whole = jnp.sum(whole, axis=0, keepdims=True)
            tail = jnp.sum(tail, axis=0, keepdims=True)
            return whole[:, 0:reach] + whole[:, 128 : 128 + reach] + tail[:, 256 : 256 + reach]

        mean = window(total, tail_total) / TAPS
        mean_square = window(square, tail_square) / TAPS
        scale_ref[c : c + 1, :] = 1.0 / (TAPS * jnp.sqrt(mean_square - mean * mean + 1e-06))


def correlate(packed_refs, distances, hankel_ref, scale_ref, moves_ref, out_len):
    each, reach = packed_refs[0].shape[0] // 3, hankel_ref.shape[2]
    per = each * 2 // 5
    combined = None
    for c in range(3):
        shaped = [unpack(ref[c * each : (c + 1) * each]) for ref in packed_refs]
        raw = jnp.dot(jnp.concatenate(shaped, axis=0), hankel_ref[c], preferred_element_type=F32)
        raw = raw * scale_ref[c : c + 1, :]
        combined = raw if combined is None else combined + raw
    row = moves_ref[...].astype(F32)
    results = []
    for n, distance in enumerate(distances):
        move = column_of(row, per, (lax.axis_index("tm") ^ distance) * per).astype(jnp.int32)
        low = jnp.broadcast_to(move & (LANES - 1), (per, LANES))
        ahead = lax.broadcasted_iota(jnp.int32, (per, LANES), 1) + low
        spot = ahead & (LANES - 1)
        inside = ahead < LANES
        far = jnp.broadcast_to(move >= LANES, (per, LANES))
        part = combined[n * per : (n + 1) * per]
        turned = [
            jnp.take_along_axis(part[:, b * LANES : (b + 1) * LANES], spot, axis=1)
            for b in range(reach // LANES)
        ]
        near = [jnp.where(inside, turned[b], turned[b + 1]) for b in range(reach // LANES - 1)]
        pieces = [jnp.where(far, near[b + 1], near[b]) for b in range(out_len // LANES)]
        results.append(jnp.concatenate(pieces, axis=1))
    return results


def own_kernel(slab_ref, following_ref, moves_ref, packed_ref, hankel_ref, scale_ref, spare_moves_ref, terms_ref):
    build_hankel(slab_ref, following_ref, hankel_ref, scale_ref)
    spare_moves_ref[...] = moves_ref[...]
    (terms_ref[...],) = correlate([packed_ref], [0], hankel_ref, scale_ref, moves_ref, terms_ref.shape[1])


def rest_kernel(distances, hankel_ref, scale_ref, moves_ref, own_ref, *refs):
    *packed_refs, keep_ref, send_ref = refs
    own = keep_ref.shape[1]
    odd = lax.axis_index("sta") % 2 == 1
    results = correlate(packed_refs, distances, hankel_ref, scale_ref, moves_ref, keep_ref.shape[2])
    for i, result in enumerate([own_ref[...]] + results):
        keep_ref[i] = jnp.where(odd, result[own:], result[:own])
        send_ref[i] = jnp.where(odd, result[:own], result[own:])


def assemble_kernel(keep_ref, arrived_ref, *out_refs):
    chip = lax.axis_index("sta") // 2
    for i in range(len(out_refs)):
        value = keep_ref[i] + arrived_ref[i]
        for j, out_ref in enumerate(out_refs):

            @pl.when(chip ^ lax.axis_index("tm") ^ i == j)
            def _():
                out_ref[...] = value


def exchange(block, axis, distance):
    return lax.ppermute(block, axis, [(i, i ^ distance) for i in range(lax.axis_size(axis))])


def per_device(records, templates, channel_mask, moveouts):
    stations, blocks = lax.axis_size("sta"), lax.axis_size("tm")
    assert stations == 2 * blocks and records.shape[0] == 1
    slab, per = records.shape[2], templates.shape[2]
    own = per // 2
    reach = slab + 2 * LANES
    masks = channel_mask.transpose(1, 0, 2)
    cost = pl.CostEstimate(flops=10**3, bytes_accessed=0, transcendentals=0)

    def call(kernel, name, *shapes):
        return pl.pallas_call(kernel, out_shape=shapes, name=name, compiler_params=SMALL, cost_estimate=cost)

    packed_shape = (3 * (2 * per + own), LANES)
    packed = pl.pallas_call(
        shape_kernel,
        out_shape=jax.ShapeDtypeStruct(packed_shape, BF16),
        in_specs=[pl.BlockSpec(memory_space=pltpu.HBM)] * 2,
        scratch_shapes=[
            pltpu.VMEM(templates.shape[1:], BF16),
            pltpu.VMEM(masks.shape, jnp.int32),
            pltpu.SemaphoreType.DMA((2,)),
        ],
        name="shape_templates",
        compiler_params=WIDE,
        cost_estimate=pl.CostEstimate(flops=10**10, bytes_accessed=0, transcendentals=0),
    )(templates[0], masks)
    library = [exchange(packed, "tm", i) for i in range(1, blocks)]
    following = lax.ppermute(records[0], "tm", [(i, i - 1) for i in range(1, blocks)])
    hankel, scale, moves, own_terms = call(
        own_kernel,
        "correlate_own",
        jax.ShapeDtypeStruct((3, TAPS_PAD, reach), BF16),
        jax.ShapeDtypeStruct((3, reach), F32),
        jax.ShapeDtypeStruct(moveouts.shape, jnp.int32),
        jax.ShapeDtypeStruct((per, slab), F32),
    )(records[0], following, moveouts, packed)
    keep, send = call(
        functools.partial(rest_kernel, range(1, blocks)),
        "correlate_rest",
        jax.ShapeDtypeStruct((blocks, own, slab), F32),
        jax.ShapeDtypeStruct((blocks, own, slab), F32),
    )(hankel, scale, moves, own_terms, *library)
    arrived = exchange(send, "sta", 1)
    piece = jax.ShapeDtypeStruct((own, slab), F32)
    chips = call(assemble_kernel, "add_cores", *[piece] * blocks)(keep, arrived)
    others = [exchange(chips[d], "sta", 2 * d) for d in range(1, blocks)]
    stacked = chips[0]
    for part in others:
        stacked = stacked + part
    return stacked


def solution(mesh):
    return jax.shard_map(
        per_device,
        mesh=mesh,
        in_specs=(
            P("sta", None, "tm"),
            P("sta", None, "tm", None),
            P("sta", None, "tm"),
            P("sta", None),
        ),
        out_specs=P("sta", "tm"),
        check_vma=False,
    )
```

time: 30.8 us -> 29.3 us (0.951)
  waiting for transfers between devices: 10.9 us -> 12.8 us
  starting transfers between devices: 12.2 us -> 10.7 us
  local copies, waits for them, and re-layouts: 2.22 us -> 0.91 us
  Pallas kernels: 4.47 us -> 4.04 us
    ppermute x1, waiting for transfers between devices: 0.01 us -> 4.42 us  [per_device(): lax.ppermute(records[0], 'tm', [(i, i - 1) for i in range(1, blocks)])]
    ppermute x8 -> x7, waiting for transfers between devices: 10.9 us -> 8.42 us  [exchange(): lax.ppermute(block, axis, [(i, i ^ distance) for i in range(lax.axis_size...]
    ppermute x8 -> x7, starting transfers between devices: 10.9 us -> 9.38 us  [exchange(): lax.ppermute(block, axis, [(i, i ^ distance) for i in range(lax.axis_size...]
    unnamed x6, local copies, waits for them, and re-layouts: 2.22 us -> 0.91 us
    pallas_call x5 -> x4, Pallas kernels: 4.47 us -> 4.04 us  [the longest x1 1.89 us: per_device(): pl.pallas_call(shape_kernel, out_shape=jax.ShapeDtypeStruct(packed_shape,...]
  transfers between devices with their start and end apart: 9 -> 8, of which waited for: 5 -> 6; matrix products, arithmetic and copies ran while one was open for 0% -> 0% of each run, Pallas kernels for 8% -> 4%
where the time goes in v2:
time: 29.3 us; the launch traced here: 29.2 us
  waiting for transfers between devices  12.8 us (44%)
  starting transfers between devices  10.7 us (37%)
  Pallas kernels  4.04 us (14%)
  local copies, waits for them, and re-layouts  0.91 us (3%)
  other arithmetic  0.65 us (2%)
    ppermute x7, starting transfers between devices, exchange(): lax.ppermute(block, axis, [(i, i ^ distance) for i in range(lax.axis_size...  9.38 us
    ppermute x7, waiting for transfers between devices, exchange(): lax.ppermute(block, axis, [(i, i ^ distance) for i in range(lax.axis_size...  8.42 us
    ppermute x1, waiting for transfers between devices, per_device(): lax.ppermute(records[0], 'tm', [(i, i - 1) for i in range(1, blocks)])  4.42 us
    pallas_call x1, Pallas kernels, per_device(): pl.pallas_call(shape_kernel, out_shape=jax.ShapeDtypeStruct(packed_shape,...  1.89 us
    ppermute x1, starting transfers between devices, per_device(): lax.ppermute(records[0], 'tm', [(i, i - 1) for i in range(1, blocks)])  1.28 us
    pallas_call x1, Pallas kernels, per_device(): call(own_kernel, 'correlate_own', jax.ShapeDtypeStruct((3, TAPS_PAD, reac...  1.13 us
    pallas_call x1, Pallas kernels, per_device(): call(functools.partial(rest_kernel, range(1, blocks)), 'correlate_rest',...  0.94 us
    unnamed x6, local copies, waits for them, and re-layouts  0.91 us
  transfers between devices with their start and end apart: 8, of which 6 were waited for; matrix products, arithmetic and copies ran while one was open for 0% of the time, Pallas kernels for 4%

profile of v2, /device:TPU:0, one launch (start us, length us, event | category | flops | bytes accessed | tf_op | source)
XLA Modules:
  0.0 29.2 jit_solution(6537570677777489331)
XLA Ops:
  0.0 0.0 copy-start.1
  0.0 0.0 copy-start.2
  0.0 1.9 %shape_templates.1.packed_ref = bf16[480,128]{1,0:T(8,128)(2,1)} custom-call(bf16[3,64,300]{2,1,0:T(8,128)(2,1)} %bitcast.5, s32[3,1,64]{2,1,0:T(1,128)} %bitcast.6), custom_call_target="tpu_custom_call" | custom-call | flops 10000000000 | tf_op jit(solution)/shard_map/shape_templates/pallas_call | solution.py:168
  1.9 5.1 %collective-permute-start.3 = (bf16[480,128]{1,0:T(8,128)(2,1)}, bf16[480,128]{1,0:T(8,128)(2,1)S(1)}, u32[]{:S(2)}, u32[]{:S(2)}) collective-permute-start(bf16[480,128]{1,0:T(8,128)(2,1)} %shape_templates.1.packed_ref), channel_id=1, source_target_pairs={{0,3},{1,2},{2,1},{3,0},{4,7},{5,6},{6,5},{7,4},{8,11},{9,10},{10,... | collective-permute-start | bytes 368648 | tf_op jit(solution)/shard_map/ppermute | solution.py:152
  7.0 0.0 collective-permute-start.2
  7.0 0.6 %collective-permute-start.1 = (bf16[480,128]{1,0:T(8,128)(2,1)}, bf16[480,128]{1,0:T(8,128)(2,1)S(1)}, u32[]{:S(2)}, u32[]{:S(2)}) collective-permute-start(bf16[480,128]{1,0:T(8,128)(2,1)} %shape_templates.1.packed_ref), channel_id=1, source_target_pairs={{0,1},{1,0},{2,3},{3,2},{4,5},{5,4},{6,7},{7,6},{8,9},{9,8},{10,11... | collective-permute-start | bytes 368648 | tf_op jit(solution)/shard_map/ppermute | solution.py:152
  7.7 0.0 copy-done.1
  7.7 1.3 %collective-permute-start = (bf16[3,512]{1,0:T(4,128)(2,1)S(1)}, bf16[3,512]{1,0:T(4,128)(2,1)S(1)}, u32[]{:S(2)}, u32[]{:S(2)}) collective-permute-start(bf16[3,512]{1,0:T(4,128)(2,1)S(1)} %bitcast.3), channel_id=1, source_target_pairs={{1,0},{2,1},{3,2},{5,4},{6,5},{7,6},{9,8},{10,9},{11,10},{13,12},{... | collective-permute-start | bytes 9224 | tf_op jit(solution)/shard_map/ppermute | solution.py:182
  8.9 4.4 %collective-permute-done.following_ref = bf16[3,512]{1,0:T(4,128)(2,1)S(1)} collective-permute-done((bf16[3,512]{1,0:T(4,128)(2,1)S(1)}, bf16[3,512]{1,0:T(4,128)(2,1)S(1)}, u32[]{:S(2)}, u32[]{:S(2)}) %collective-permute-start) | collective-permute-done | bytes 3104 | tf_op jit(solution)/shard_map/ppermute | solution.py:182
  13.4 0.0 copy-done.2
  13.4 0.0 copy-start
  13.4 0.9 %copy-done = bf16[480,128]{1,0:T(8,128)(2,1)S(1)} copy-done((bf16[480,128]{1,0:T(8,128)(2,1)S(1)}, bf16[480,128]{1,0:T(8,128)(2,1)}, u32[]{:S(2)}) %copy-start) | copy-done | bytes 122904
  14.3 1.1 %correlate_own.1 = (bf16[3,384,768]{2,1,0:T(8,128)(2,1)S(1)}, f32[3,768]{1,0:T(4,128)S(1)}, s32[1,256]{1,0:T(1,128)S(1)}, f32[64,512]{1,0:T(8,128)S(1)}) custom-call(bf16[3,512]{1,0:T(4,128)(2,1)S(1)} %bitcast.4, bf16[3,512]{1,0:T(4,128)(2,1)S(1)} %collective-permute-done.following_ref, s32[1,256]{1,0:T(1,128)S(1)} %copy-done.2, bf16[480,128]{1,0:T(8,128)(2,1)S(1)} %copy-done), custom_call_target="tpu_custom_call" | custom-call | flops 1000 | tf_op jit(solution)/shard_map/correlate_own/pallas_call | solution.py:183
  15.4 0.0 collective-permute-done.3.refs_2_
  15.4 2.2 %collective-permute-done.2.refs_1_ = bf16[480,128]{1,0:T(8,128)(2,1)S(1)} collective-permute-done((bf16[480,128]{1,0:T(8,128)(2,1)}, bf16[480,128]{1,0:T(8,128)(2,1)S(1)}, u32[]{:S(2)}, u32[]{:S(2)}) %collective-permute-start.2) | collective-permute-done | bytes 122912 | tf_op jit(solution)/shard_map/ppermute | solution.py:152
  17.6 0.0 collective-permute-done.1.refs_0_
  17.6 0.9 %correlate_rest.1 = (f32[4,32,512]{2,1,0:T(8,128)S(1)}, f32[4,32,512]{2,1,0:T(8,128)S(1)}) custom-call(bf16[3,384,768]{2,1,0:T(8,128)(2,1)S(1)} %get-tuple-element.15.hankel_ref, f32[3,768]{1,0:T(4,128)S(1)} %get-tuple-element.16.scale_ref, s32[1,256]{1,0:T(1,128)S(1)} %get-tuple-element.17.moves_ref, f32[64,512]{1,0:T(8,128)S(1)} %get-tuple-element.18.own_ref, ...), custom_call_target="tpu_custom_call" | custom-call | flops 1000 | tf_op jit(solution)/shard_map/correlate_rest/pallas_call | solution.py:191
  18.6 0.1 collective-permute-start.4
  18.7 1.5 %collective-permute-done.4.arrived_ref = f32[4,32,512]{2,1,0:T(8,128)S(1)} collective-permute-done((f32[4,32,512]{2,1,0:T(8,128)S(1)}, f32[4,32,512]{2,1,0:T(8,128)S(1)}, u32[]{:S(2)}, u32[]{:S(2)}) %collective-permute-start.4) | collective-permute-done | bytes 262176 | tf_op jit(solution)/shard_map/ppermute | solution.py:152
  20.2 0.1 add_cores.1
  20.3 1.6 %collective-permute-start.5 = (f32[32,512]{1,0:T(8,128)S(1)}, f32[32,512]{1,0:T(8,128)S(1)}, u32[]{:S(2)}, u32[]{:S(2)}) collective-permute-start(f32[32,512]{1,0:T(8,128)S(1)} %get-tuple-element.22), channel_id=1, source_target_pairs={{0,8},{4,12},{8,0},{12,4},{16,24},{20,28},{24,16},{28,20},{1,9},{5... | collective-permute-start | bytes 196616 | tf_op jit(solution)/shard_map/ppermute | solution.py:152
  21.8 1.5 %collective-permute-start.6 = (f32[32,512]{1,0:T(8,128)S(1)}, f32[32,512]{1,0:T(8,128)S(1)}, u32[]{:S(2)}, u32[]{:S(2)}) collective-permute-start(f32[32,512]{1,0:T(8,128)S(1)} %get-tuple-element.23), channel_id=1, source_target_pairs={{0,16},{4,20},{8,24},{12,28},{16,0},{20,4},{24,8},{28,12},{1,17},{... | collective-permute-start | bytes 196616 | tf_op jit(solution)/shard_map/ppermute | solution.py:152
  23.3 0.5 %collective-permute-start.7 = (f32[32,512]{1,0:T(8,128)S(1)}, f32[32,512]{1,0:T(8,128)S(1)}, u32[]{:S(2)}, u32[]{:S(2)}) collective-permute-start(f32[32,512]{1,0:T(8,128)S(1)} %get-tuple-element.24), channel_id=1, source_target_pairs={{0,24},{4,28},{8,16},{12,20},{16,8},{20,12},{24,0},{28,4},{1,25},{... | collective-permute-start | bytes 196616 | tf_op jit(solution)/shard_map/ppermute | solution.py:152
  23.8 0.8 %collective-permute-done.5 = f32[32,512]{1,0:T(8,128)S(1)} collective-permute-done((f32[32,512]{1,0:T(8,128)S(1)}, f32[32,512]{1,0:T(8,128)S(1)}, u32[]{:S(2)}, u32[]{:S(2)}) %collective-permute-start.5) | collective-permute-done | bytes 65568 | tf_op jit(solution)/shard_map/ppermute | solution.py:152
  24.6 1.5 %collective-permute-done.6 = f32[32,512]{1,0:T(8,128)S(1)} collective-permute-done((f32[32,512]{1,0:T(8,128)S(1)}, f32[32,512]{1,0:T(8,128)S(1)}, u32[]{:S(2)}, u32[]{:S(2)}) %collective-permute-start.6) | collective-permute-done | bytes 65568 | tf_op jit(solution)/shard_map/ppermute | solution.py:152
  26.1 2.4 %collective-permute-done.7 = f32[32,512]{1,0:T(8,128)S(1)} collective-permute-done((f32[32,512]{1,0:T(8,128)S(1)}, f32[32,512]{1,0:T(8,128)S(1)}, u32[]{:S(2)}, u32[]{:S(2)}) %collective-permute-start.7) | collective-permute-done | bytes 65568 | tf_op jit(solution)/shard_map/ppermute | solution.py:152
  28.5 0.6 %add_add_fusion = f32[32,512]{1,0:T(8,128)} fusion(f32[32,512]{1,0:T(8,128)S(1)} %collective-permute-done.7, f32[32,512]{1,0:T(8,128)S(1)} %collective-permute-done.6, f32[32,512]{1,0:T(8,128)S(1)} %get-tuple-element.21, f32[32,512]{1,0:T(8,128)S(1)} %collective-permute-done.5), kind=kLoop, calls=%fused_computation | loop fusion | flops 49152 | bytes 327680 | tf_op jit(solution)/shard_map/add | solution.py:203
Async XLA Ops:
  0.0 7.7 %copy-start.1 = (bf16[1,3,512]{2,1,0:T(4,128)(2,1)S(1)}, bf16[1,3,512]{2,1,0:T(4,128)(2,1)}, u32[]{:S(2)}) copy-start(bf16[1,3,512]{2,1,0:T(4,128)(2,1)} %param.4) | copy-start | bytes 9220
  0.0 13.4 %copy-start.2 = (s32[1,256]{1,0:T(1,128)S(1)}, s32[1,256]{1,0:T(1,128)}, u32[]{:S(2)}) copy-start(s32[1,256]{1,0:T(1,128)} %moves_ref.1) | copy-start | bytes 3076
  1.9 13.5 %collective-permute-start.3 = (bf16[480,128]{1,0:T(8,128)(2,1)}, bf16[480,128]{1,0:T(8,128)(2,1)S(1)}, u32[]{:S(2)}, u32[]{:S(2)}) collective-permute-start(bf16[480,128]{1,0:T(8,128)(2,1)} %shape_templates.1.packed_ref), channel_id=1, source_target_pairs={{0,3},{1,2},{2,1},{3,0},{4,7},{5,6},{6,5},{7,4},{8,11},{9,10},{10,... | collective-permute-start | bytes 368648 | tf_op jit(solution)/shard_map/ppermute | solution.py:152
  7.0 10.6 %collective-permute-start.2 = (bf16[480,128]{1,0:T(8,128)(2,1)}, bf16[480,128]{1,0:T(8,128)(2,1)S(1)}, u32[]{:S(2)}, u32[]{:S(2)}) collective-permute-start(bf16[480,128]{1,0:T(8,128)(2,1)} %shape_templates.1.packed_ref), channel_id=1, source_target_pairs={{0,2},{1,3},{2,0},{3,1},{4,6},{5,7},{6,4},{7,5},{8,10},{9,11},{10,... | collective-permute-start | bytes 368648 | tf_op jit(solution)/shard_map/ppermute | solution.py:152
  7.0 10.6 %collective-permute-start.1 = (bf16[480,128]{1,0:T(8,128)(2,1)}, bf16[480,128]{1,0:T(8,128)(2,1)S(1)}, u32[]{:S(2)}, u32[]{:S(2)}) collective-permute-start(bf16[480,128]{1,0:T(8,128)(2,1)} %shape_templates.1.packed_ref), channel_id=1, source_target_pairs={{0,1},{1,0},{2,3},{3,2},{4,5},{5,4},{6,7},{7,6},{8,9},{9,8},{10,11... | collective-permute-start | bytes 368648 | tf_op jit(solution)/shard_map/ppermute | solution.py:152
  7.7 5.7 %collective-permute-start = (bf16[3,512]{1,0:T(4,128)(2,1)S(1)}, bf16[3,512]{1,0:T(4,128)(2,1)S(1)}, u32[]{:S(2)}, u32[]{:S(2)}) collective-permute-start(bf16[3,512]{1,0:T(4,128)(2,1)S(1)} %bitcast.3), channel_id=1, source_target_pairs={{1,0},{2,1},{3,2},{5,4},{6,5},{7,6},{9,8},{10,9},{11,10},{13,12},{... | collective-permute-start | bytes 9224 | tf_op jit(solution)/shard_map/ppermute | solution.py:182
  13.4 0.9 %copy-start = (bf16[480,128]{1,0:T(8,128)(2,1)S(1)}, bf16[480,128]{1,0:T(8,128)(2,1)}, u32[]{:S(2)}) copy-start(bf16[480,128]{1,0:T(8,128)(2,1)} %shape_templates.1.packed_ref) | copy-start | bytes 368644
  18.6 1.6 %collective-permute-start.4 = (f32[4,32,512]{2,1,0:T(8,128)S(1)}, f32[4,32,512]{2,1,0:T(8,128)S(1)}, u32[]{:S(2)}, u32[]{:S(2)}) collective-permute-start(f32[4,32,512]{2,1,0:T(8,128)S(1)} %get-tuple-element.20), channel_id=1, source_target_pairs={{0,4},{4,0},{8,12},{12,8},{16,20},{20,16},{24,28},{28,24},{1,5},{5... | collective-permute-start | bytes 786440 | tf_op jit(solution)/shard_map/ppermute | solution.py:152
  20.3 4.3 %collective-permute-start.5 = (f32[32,512]{1,0:T(8,128)S(1)}, f32[32,512]{1,0:T(8,128)S(1)}, u32[]{:S(2)}, u32[]{:S(2)}) collective-permute-start(f32[32,512]{1,0:T(8,128)S(1)} %get-tuple-element.22), channel_id=1, source_target_pairs={{0,8},{4,12},{8,0},{12,4},{16,24},{20,28},{24,16},{28,20},{1,9},{5... | collective-permute-start | bytes 196616 | tf_op jit(solution)/shard_map/ppermute | solution.py:152
  21.8 4.3 %collective-permute-start.6 = (f32[32,512]{1,0:T(8,128)S(1)}, f32[32,512]{1,0:T(8,128)S(1)}, u32[]{:S(2)}, u32[]{:S(2)}) collective-permute-start(f32[32,512]{1,0:T(8,128)S(1)} %get-tuple-element.23), channel_id=1, source_target_pairs={{0,16},{4,20},{8,24},{12,28},{16,0},{20,4},{24,8},{28,12},{1,17},{... | collective-permute-start | bytes 196616 | tf_op jit(solution)/shard_map/ppermute | solution.py:152
  23.3 5.2 %collective-permute-start.7 = (f32[32,512]{1,0:T(8,128)S(1)}, f32[32,512]{1,0:T(8,128)S(1)}, u32[]{:S(2)}, u32[]{:S(2)}) collective-permute-start(f32[32,512]{1,0:T(8,128)S(1)} %get-tuple-element.24), channel_id=1, source_target_pairs={{0,24},{4,28},{8,16},{12,20},{16,8},{20,12},{24,0},{28,4},{1,25},{... | collective-permute-start | bytes 196616 | tf_op jit(solution)/shard_map/ppermute | solution.py:152

commit v3 on v2

--- a/solution.py
+++ b/solution.py
@@ -197,7 +197,7 @@
     arrived = exchange(send, "sta", 1)
     piece = jax.ShapeDtypeStruct((own, slab), F32)
     chips = call(assemble_kernel, "add_cores", *[piece] * blocks)(keep, arrived)
-    others = [exchange(chips[d], "sta", 2 * d) for d in range(1, blocks)]
+    others = [exchange(chips[d], "sta", 2 * d) for d in range(blocks - 1, 0, -1)]
     stacked = chips[0]
     for part in others:
         stacked = stacked + part

time: 29.3 us -> 28.4 us (0.969)
  waiting for transfers between devices: 12.8 us -> 11.9 us
    ppermute x7, waiting for transfers between devices: 8.42 us -> 7.47 us  [exchange(): lax.ppermute(block, axis, [(i, i ^ distance) for i in range(lax.axis_size...]
where the time goes in v3:
time: 28.4 us; the launch traced here: 28.2 us
  waiting for transfers between devices  11.9 us (42%)
  starting transfers between devices  10.7 us (38%)
  Pallas kernels  4.04 us (14%)
  local copies, waits for them, and re-layouts  0.91 us (3%)
  other arithmetic  0.65 us (2%)
    ppermute x7, starting transfers between devices, exchange(): lax.ppermute(block, axis, [(i, i ^ distance) for i in range(lax.axis_size...  9.38 us
    ppermute x7, waiting for transfers between devices, exchange(): lax.ppermute(block, axis, [(i, i ^ distance) for i in range(lax.axis_size...  7.47 us
    ppermute x1, waiting for transfers between devices, per_device(): lax.ppermute(records[0], 'tm', [(i, i - 1) for i in range(1, blocks)])  4.42 us
    pallas_call x1, Pallas kernels, per_device(): pl.pallas_call(shape_kernel, out_shape=jax.ShapeDtypeStruct(packed_shape,...  1.89 us
    ppermute x1, starting transfers between devices, per_device(): lax.ppermute(records[0], 'tm', [(i, i - 1) for i in range(1, blocks)])  1.28 us
    pallas_call x1, Pallas kernels, per_device(): call(own_kernel, 'correlate_own', jax.ShapeDtypeStruct((3, TAPS_PAD, reac...  1.13 us
    pallas_call x1, Pallas kernels, per_device(): call(functools.partial(rest_kernel, range(1, blocks)), 'correlate_rest',...  0.94 us
    unnamed x6, local copies, waits for them, and re-layouts  0.91 us
  transfers between devices with their start and end apart: 8, of which 6 were waited for; matrix products, arithmetic and copies ran while one was open for 0% of the time, Pallas kernels for 4%

profile of v3, /device:TPU:0, one launch (start us, length us, event | category | flops | bytes accessed | tf_op | source)
XLA Modules:
  0.0 28.2 jit_solution(1298921140494586211)
XLA Ops:
  0.0 0.0 copy-start.1
  0.0 0.0 copy-start.2
  0.0 1.9 %shape_templates.1.packed_ref = bf16[480,128]{1,0:T(8,128)(2,1)} custom-call(bf16[3,64,300]{2,1,0:T(8,128)(2,1)} %bitcast.5, s32[3,1,64]{2,1,0:T(1,128)} %bitcast.6), custom_call_target="tpu_custom_call" | custom-call | flops 10000000000 | tf_op jit(solution)/shard_map/shape_templates/pallas_call | solution.py:168
  1.9 5.1 %collective-permute-start.3 = (bf16[480,128]{1,0:T(8,128)(2,1)}, bf16[480,128]{1,0:T(8,128)(2,1)S(1)}, u32[]{:S(2)}, u32[]{:S(2)}) collective-permute-start(bf16[480,128]{1,0:T(8,128)(2,1)} %shape_templates.1.packed_ref), channel_id=1, source_target_pairs={{0,3},{1,2},{2,1},{3,0},{4,7},{5,6},{6,5},{7,4},{8,11},{9,10},{10,... | collective-permute-start | bytes 368648 | tf_op jit(solution)/shard_map/ppermute | solution.py:152
  7.0 0.0 collective-permute-start.2
  7.0 0.6 %collective-permute-start.1 = (bf16[480,128]{1,0:T(8,128)(2,1)}, bf16[480,128]{1,0:T(8,128)(2,1)S(1)}, u32[]{:S(2)}, u32[]{:S(2)}) collective-permute-start(bf16[480,128]{1,0:T(8,128)(2,1)} %shape_templates.1.packed_ref), channel_id=1, source_target_pairs={{0,1},{1,0},{2,3},{3,2},{4,5},{5,4},{6,7},{7,6},{8,9},{9,8},{10,11... | collective-permute-start | bytes 368648 | tf_op jit(solution)/shard_map/ppermute | solution.py:152
  7.7 0.0 copy-done.1
  7.7 1.3 %collective-permute-start = (bf16[3,512]{1,0:T(4,128)(2,1)S(1)}, bf16[3,512]{1,0:T(4,128)(2,1)S(1)}, u32[]{:S(2)}, u32[]{:S(2)}) collective-permute-start(bf16[3,512]{1,0:T(4,128)(2,1)S(1)} %bitcast.3), channel_id=1, source_target_pairs={{1,0},{2,1},{3,2},{5,4},{6,5},{7,6},{9,8},{10,9},{11,10},{13,12},{... | collective-permute-start | bytes 9224 | tf_op jit(solution)/shard_map/ppermute | solution.py:182
  8.9 4.4 %collective-permute-done.following_ref = bf16[3,512]{1,0:T(4,128)(2,1)S(1)} collective-permute-done((bf16[3,512]{1,0:T(4,128)(2,1)S(1)}, bf16[3,512]{1,0:T(4,128)(2,1)S(1)}, u32[]{:S(2)}, u32[]{:S(2)}) %collective-permute-start) | collective-permute-done | bytes 3104 | tf_op jit(solution)/shard_map/ppermute | solution.py:182
  13.4 0.0 copy-done.2
  13.4 0.0 copy-start
  13.4 0.9 %copy-done = bf16[480,128]{1,0:T(8,128)(2,1)S(1)} copy-done((bf16[480,128]{1,0:T(8,128)(2,1)S(1)}, bf16[480,128]{1,0:T(8,128)(2,1)}, u32[]{:S(2)}) %copy-start) | copy-done | bytes 122904
  14.3 1.1 %correlate_own.1 = (bf16[3,384,768]{2,1,0:T(8,128)(2,1)S(1)}, f32[3,768]{1,0:T(4,128)S(1)}, s32[1,256]{1,0:T(1,128)S(1)}, f32[64,512]{1,0:T(8,128)S(1)}) custom-call(bf16[3,512]{1,0:T(4,128)(2,1)S(1)} %bitcast.4, bf16[3,512]{1,0:T(4,128)(2,1)S(1)} %collective-permute-done.following_ref, s32[1,256]{1,0:T(1,128)S(1)} %copy-done.2, bf16[480,128]{1,0:T(8,128)(2,1)S(1)} %copy-done), custom_call_target="tpu_custom_call" | custom-call | flops 1000 | tf_op jit(solution)/shard_map/correlate_own/pallas_call | solution.py:183
  15.4 0.0 collective-permute-done.3.refs_2_
  15.4 2.2 %collective-permute-done.2.refs_1_ = bf16[480,128]{1,0:T(8,128)(2,1)S(1)} collective-permute-done((bf16[480,128]{1,0:T(8,128)(2,1)}, bf16[480,128]{1,0:T(8,128)(2,1)S(1)}, u32[]{:S(2)}, u32[]{:S(2)}) %collective-permute-start.2) | collective-permute-done | bytes 122912 | tf_op jit(solution)/shard_map/ppermute | solution.py:152
  17.6 0.0 collective-permute-done.1.refs_0_
  17.6 0.9 %correlate_rest.1 = (f32[4,32,512]{2,1,0:T(8,128)S(1)}, f32[4,32,512]{2,1,0:T(8,128)S(1)}) custom-call(bf16[3,384,768]{2,1,0:T(8,128)(2,1)S(1)} %get-tuple-element.15.hankel_ref, f32[3,768]{1,0:T(4,128)S(1)} %get-tuple-element.16.scale_ref, s32[1,256]{1,0:T(1,128)S(1)} %get-tuple-element.17.moves_ref, f32[64,512]{1,0:T(8,128)S(1)} %get-tuple-element.18.own_ref, ...), custom_call_target="tpu_custom_call" | custom-call | flops 1000 | tf_op jit(solution)/shard_map/correlate_rest/pallas_call | solution.py:191
  18.6 0.1 collective-permute-start.4
  18.7 1.5 %collective-permute-done.4.arrived_ref = f32[4,32,512]{2,1,0:T(8,128)S(1)} collective-permute-done((f32[4,32,512]{2,1,0:T(8,128)S(1)}, f32[4,32,512]{2,1,0:T(8,128)S(1)}, u32[]{:S(2)}, u32[]{:S(2)}) %collective-permute-start.4) | collective-permute-done | bytes 262176 | tf_op jit(solution)/shard_map/ppermute | solution.py:152
  20.2 0.1 add_cores.1
  20.3 2.5 %collective-permute-start.5 = (f32[32,512]{1,0:T(8,128)S(1)}, f32[32,512]{1,0:T(8,128)S(1)}, u32[]{:S(2)}, u32[]{:S(2)}) collective-permute-start(f32[32,512]{1,0:T(8,128)S(1)} %get-tuple-element.22), channel_id=1, source_target_pairs={{0,24},{4,28},{8,16},{12,20},{16,8},{20,12},{24,0},{28,4},{1,25},{... | collective-permute-start | bytes 196616 | tf_op jit(solution)/shard_map/ppermute | solution.py:152
  22.8 0.5 %collective-permute-start.6 = (f32[32,512]{1,0:T(8,128)S(1)}, f32[32,512]{1,0:T(8,128)S(1)}, u32[]{:S(2)}, u32[]{:S(2)}) collective-permute-start(f32[32,512]{1,0:T(8,128)S(1)} %get-tuple-element.23), channel_id=1, source_target_pairs={{0,16},{4,20},{8,24},{12,28},{16,0},{20,4},{24,8},{28,12},{1,17},{... | collective-permute-start | bytes 196616 | tf_op jit(solution)/shard_map/ppermute | solution.py:152
  23.3 0.5 %collective-permute-start.7 = (f32[32,512]{1,0:T(8,128)S(1)}, f32[32,512]{1,0:T(8,128)S(1)}, u32[]{:S(2)}, u32[]{:S(2)}) collective-permute-start(f32[32,512]{1,0:T(8,128)S(1)} %get-tuple-element.24), channel_id=1, source_target_pairs={{0,8},{4,12},{8,0},{12,4},{16,24},{20,28},{24,16},{28,20},{1,9},{5... | collective-permute-start | bytes 196616 | tf_op jit(solution)/shard_map/ppermute | solution.py:152
  23.8 1.7 %collective-permute-done.5 = f32[32,512]{1,0:T(8,128)S(1)} collective-permute-done((f32[32,512]{1,0:T(8,128)S(1)}, f32[32,512]{1,0:T(8,128)S(1)}, u32[]{:S(2)}, u32[]{:S(2)}) %collective-permute-start.5) | collective-permute-done | bytes 65568 | tf_op jit(solution)/shard_map/ppermute | solution.py:152
  25.5 1.5 %collective-permute-done.6 = f32[32,512]{1,0:T(8,128)S(1)} collective-permute-done((f32[32,512]{1,0:T(8,128)S(1)}, f32[32,512]{1,0:T(8,128)S(1)}, u32[]{:S(2)}, u32[]{:S(2)}) %collective-permute-start.6) | collective-permute-done | bytes 65568 | tf_op jit(solution)/shard_map/ppermute | solution.py:152
  27.0 0.5 %collective-permute-done.7 = f32[32,512]{1,0:T(8,128)S(1)} collective-permute-done((f32[32,512]{1,0:T(8,128)S(1)}, f32[32,512]{1,0:T(8,128)S(1)}, u32[]{:S(2)}, u32[]{:S(2)}) %collective-permute-start.7) | collective-permute-done | bytes 65568 | tf_op jit(solution)/shard_map/ppermute | solution.py:152
  27.6 0.6 %add_add_fusion = f32[32,512]{1,0:T(8,128)} fusion(f32[32,512]{1,0:T(8,128)S(1)} %collective-permute-done.7, f32[32,512]{1,0:T(8,128)S(1)} %collective-permute-done.6, f32[32,512]{1,0:T(8,128)S(1)} %get-tuple-element.21, f32[32,512]{1,0:T(8,128)S(1)} %collective-permute-done.5), kind=kLoop, calls=%fused_computation | loop fusion | flops 49152 | bytes 327680 | tf_op jit(solution)/shard_map/add | solution.py:203
Async XLA Ops:
  0.0 7.7 %copy-start.1 = (bf16[1,3,512]{2,1,0:T(4,128)(2,1)S(1)}, bf16[1,3,512]{2,1,0:T(4,128)(2,1)}, u32[]{:S(2)}) copy-start(bf16[1,3,512]{2,1,0:T(4,128)(2,1)} %param.4) | copy-start | bytes 9220
  0.0 13.4 %copy-start.2 = (s32[1,256]{1,0:T(1,128)S(1)}, s32[1,256]{1,0:T(1,128)}, u32[]{:S(2)}) copy-start(s32[1,256]{1,0:T(1,128)} %moves_ref.1) | copy-start | bytes 3076
  1.9 13.5 %collective-permute-start.3 = (bf16[480,128]{1,0:T(8,128)(2,1)}, bf16[480,128]{1,0:T(8,128)(2,1)S(1)}, u32[]{:S(2)}, u32[]{:S(2)}) collective-permute-start(bf16[480,128]{1,0:T(8,128)(2,1)} %shape_templates.1.packed_ref), channel_id=1, source_target_pairs={{0,3},{1,2},{2,1},{3,0},{4,7},{5,6},{6,5},{7,4},{8,11},{9,10},{10,... | collective-permute-start | bytes 368648 | tf_op jit(solution)/shard_map/ppermute | solution.py:152
  7.0 10.6 %collective-permute-start.2 = (bf16[480,128]{1,0:T(8,128)(2,1)}, bf16[480,128]{1,0:T(8,128)(2,1)S(1)}, u32[]{:S(2)}, u32[]{:S(2)}) collective-permute-start(bf16[480,128]{1,0:T(8,128)(2,1)} %shape_templates.1.packed_ref), channel_id=1, source_target_pairs={{0,2},{1,3},{2,0},{3,1},{4,6},{5,7},{6,4},{7,5},{8,10},{9,11},{10,... | collective-permute-start | bytes 368648 | tf_op jit(solution)/shard_map/ppermute | solution.py:152
  7.0 10.6 %collective-permute-start.1 = (bf16[480,128]{1,0:T(8,128)(2,1)}, bf16[480,128]{1,0:T(8,128)(2,1)S(1)}, u32[]{:S(2)}, u32[]{:S(2)}) collective-permute-start(bf16[480,128]{1,0:T(8,128)(2,1)} %shape_templates.1.packed_ref), channel_id=1, source_target_pairs={{0,1},{1,0},{2,3},{3,2},{4,5},{5,4},{6,7},{7,6},{8,9},{9,8},{10,11... | collective-permute-start | bytes 368648 | tf_op jit(solution)/shard_map/ppermute | solution.py:152
  7.7 5.7 %collective-permute-start = (bf16[3,512]{1,0:T(4,128)(2,1)S(1)}, bf16[3,512]{1,0:T(4,128)(2,1)S(1)}, u32[]{:S(2)}, u32[]{:S(2)}) collective-permute-start(bf16[3,512]{1,0:T(4,128)(2,1)S(1)} %bitcast.3), channel_id=1, source_target_pairs={{1,0},{2,1},{3,2},{5,4},{6,5},{7,6},{9,8},{10,9},{11,10},{13,12},{... | collective-permute-start | bytes 9224 | tf_op jit(solution)/shard_map/ppermute | solution.py:182
  13.4 0.9 %copy-start = (bf16[480,128]{1,0:T(8,128)(2,1)S(1)}, bf16[480,128]{1,0:T(8,128)(2,1)}, u32[]{:S(2)}) copy-start(bf16[480,128]{1,0:T(8,128)(2,1)} %shape_templates.1.packed_ref) | copy-start | bytes 368644
  18.6 1.6 %collective-permute-start.4 = (f32[4,32,512]{2,1,0:T(8,128)S(1)}, f32[4,32,512]{2,1,0:T(8,128)S(1)}, u32[]{:S(2)}, u32[]{:S(2)}) collective-permute-start(f32[4,32,512]{2,1,0:T(8,128)S(1)} %get-tuple-element.20), channel_id=1, source_target_pairs={{0,4},{4,0},{8,12},{12,8},{16,20},{20,16},{24,28},{28,24},{1,5},{5... | collective-permute-start | bytes 786440 | tf_op jit(solution)/shard_map/ppermute | solution.py:152
  20.3 5.3 %collective-permute-start.5 = (f32[32,512]{1,0:T(8,128)S(1)}, f32[32,512]{1,0:T(8,128)S(1)}, u32[]{:S(2)}, u32[]{:S(2)}) collective-permute-start(f32[32,512]{1,0:T(8,128)S(1)} %get-tuple-element.22), channel_id=1, source_target_pairs={{0,24},{4,28},{8,16},{12,20},{16,8},{20,12},{24,0},{28,4},{1,25},{... | collective-permute-start | bytes 196616 | tf_op jit(solution)/shard_map/ppermute | solution.py:152
  22.8 4.3 %collective-permute-start.6 = (f32[32,512]{1,0:T(8,128)S(1)}, f32[32,512]{1,0:T(8,128)S(1)}, u32[]{:S(2)}, u32[]{:S(2)}) collective-permute-start(f32[32,512]{1,0:T(8,128)S(1)} %get-tuple-element.23), channel_id=1, source_target_pairs={{0,16},{4,20},{8,24},{12,28},{16,0},{20,4},{24,8},{28,12},{1,17},{... | collective-permute-start | bytes 196616 | tf_op jit(solution)/shard_map/ppermute | solution.py:152
  23.3 4.3 %collective-permute-start.7 = (f32[32,512]{1,0:T(8,128)S(1)}, f32[32,512]{1,0:T(8,128)S(1)}, u32[]{:S(2)}, u32[]{:S(2)}) collective-permute-start(f32[32,512]{1,0:T(8,128)S(1)} %get-tuple-element.24), channel_id=1, source_target_pairs={{0,8},{4,12},{8,0},{12,4},{16,24},{20,28},{24,16},{28,20},{1,9},{5... | collective-permute-start | bytes 196616 | tf_op jit(solution)/shard_map/ppermute | solution.py:152

commit v4 on v3

--- a/solution.py
+++ b/solution.py
@@ -12,7 +12,7 @@
 F32 = jnp.float32
 BF16 = jnp.bfloat16
 SMALL = pltpu.CompilerParams(vmem_limit_bytes=16 << 20)
-WIDE = pltpu.CompilerParams(vmem_limit_bytes=60 << 20)
+COST = {"table": 10**10}
 
 
 def column_of(row, rows, first):
@@ -23,23 +23,21 @@
     return jnp.sum(jnp.where(at, wide, jnp.zeros_like(wide)), axis=1, keepdims=True)
 
 
-def shape_kernel(templates_hbm, mask_hbm, packed_ref, templates_ref, mask_ref, sems):
+def table_kernel(table_ref):
+    shape = table_ref.shape
+    at = lax.broadcasted_iota(jnp.int32, shape, 0) == lax.broadcasted_iota(jnp.int32, shape, 1)
+    table_ref[...] = at.astype(F32)
+
+
+def shape_kernel(table_ref, templates_ref, mask_ref, packed_ref):
     per = templates_ref.shape[1]
     each = packed_ref.shape[0] // 3
-    copies = [
-        pltpu.make_async_copy(mask_hbm, mask_ref, sems.at[0]),
-        pltpu.make_async_copy(templates_hbm, templates_ref, sems.at[1]),
-    ]
-    for copy in copies:
-        copy.start()
-    for copy in copies:
-        copy.wait()
     for c in range(3):
         values = templates_ref[c].astype(F32)
         center = jnp.sum(values, axis=1, keepdims=True) / TAPS
         spread = values - center
         rms = jnp.sqrt(jnp.sum(spread * spread, axis=1, keepdims=True) / TAPS + 1e-06)
-        weight = column_of(mask_ref[c].astype(F32), per, 0)
+        weight = jnp.sum(table_ref[...] * mask_ref[c].astype(F32), axis=1, keepdims=True)
         shaped = spread / rms * weight
         tail = jnp.concatenate([shaped[:, 256:TAPS], jnp.zeros((per, TAPS_PAD - TAPS), F32)], axis=1)
         tail = tail[: per // 2] + pltpu.roll(tail[per // 2 :], 64, 1)
@@ -127,23 +125,35 @@
     (terms_ref[...],) = correlate([packed_ref], [0], hankel_ref, scale_ref, moves_ref, terms_ref.shape[1])
 
 
-def rest_kernel(distances, hankel_ref, scale_ref, moves_ref, own_ref, *refs):
-    *packed_refs, keep_ref, send_ref = refs
+def store_halves(results, keep_ref, send_ref, first):
     own = keep_ref.shape[1]
     odd = lax.axis_index("sta") % 2 == 1
+    for i, result in enumerate(results):
+        keep_ref[first + i] = jnp.where(odd, result[own:], result[:own])
+        send_ref[first + i] = jnp.where(odd, result[:own], result[own:])
+
+
+def early_kernel(distances, hankel_ref, scale_ref, moves_ref, own_ref, *refs):
+    *packed_refs, keep_ref, send_ref = refs
     results = correlate(packed_refs, distances, hankel_ref, scale_ref, moves_ref, keep_ref.shape[2])
-    for i, result in enumerate([own_ref[...]] + results):
-        keep_ref[i] = jnp.where(odd, result[own:], result[:own])
-        send_ref[i] = jnp.where(odd, result[:own], result[own:])
-
-
-def assemble_kernel(keep_ref, arrived_ref, *out_refs):
+    store_halves([own_ref[...]] + results, keep_ref, send_ref, 0)
+
+
+def last_kernel(distance, hankel_ref, scale_ref, moves_ref, early_keep_ref, early_send_ref, packed_ref, keep_ref, send_ref):
+    early = early_keep_ref.shape[0]
+    keep_ref[0:early] = early_keep_ref[...]
+    send_ref[0:early] = early_send_ref[...]
+    results = correlate([packed_ref], [distance], hankel_ref, scale_ref, moves_ref, keep_ref.shape[2])
+    store_halves(results, keep_ref, send_ref, early)
+
+
+def assemble_kernel(distances, keep_ref, arrived_ref, *out_refs):
     chip = lax.axis_index("sta") // 2
-    for i in range(len(out_refs)):
+    for i, distance in enumerate(distances):
         value = keep_ref[i] + arrived_ref[i]
         for j, out_ref in enumerate(out_refs):
 
-            @pl.when(chip ^ lax.axis_index("tm") ^ i == j)
+            @pl.when(chip ^ lax.axis_index("tm") ^ distance == j)
             def _():
                 out_ref[...] = value
 
@@ -159,26 +169,18 @@
     own = per // 2
     reach = slab + 2 * LANES
     masks = channel_mask.transpose(1, 0, 2)
-    cost = pl.CostEstimate(flops=10**3, bytes_accessed=0, transcendentals=0)
 
     def call(kernel, name, *shapes):
+        cost = pl.CostEstimate(flops=COST.get(name, 10**3), bytes_accessed=0, transcendentals=0)
         return pl.pallas_call(kernel, out_shape=shapes, name=name, compiler_params=SMALL, cost_estimate=cost)
 
     packed_shape = (3 * (2 * per + own), LANES)
-    packed = pl.pallas_call(
-        shape_kernel,
-        out_shape=jax.ShapeDtypeStruct(packed_shape, BF16),
-        in_specs=[pl.BlockSpec(memory_space=pltpu.HBM)] * 2,
-        scratch_shapes=[
-            pltpu.VMEM(templates.shape[1:], BF16),
-            pltpu.VMEM(masks.shape, jnp.int32),
-            pltpu.SemaphoreType.DMA((2,)),
-        ],
-        name="shape_templates",
-        compiler_params=WIDE,
-        cost_estimate=pl.CostEstimate(flops=10**10, bytes_accessed=0, transcendentals=0),
-    )(templates[0], masks)
-    library = [exchange(packed, "tm", i) for i in range(1, blocks)]
+    (table,) = call(table_kernel, "table", jax.ShapeDtypeStruct((per, per), F32))()
+    (packed,) = call(shape_kernel, "shape_templates", jax.ShapeDtypeStruct(packed_shape, BF16))(
+        table, templates[0], masks
+    )
+    distances = list(range(blocks))
+    library = [exchange(packed, "tm", i) for i in distances[1:]]
     following = lax.ppermute(records[0], "tm", [(i, i - 1) for i in range(1, blocks)])
     hankel, scale, moves, own_terms = call(
         own_kernel,
@@ -188,15 +190,17 @@
         jax.ShapeDtypeStruct(moveouts.shape, jnp.int32),
         jax.ShapeDtypeStruct((per, slab), F32),
     )(records[0], following, moveouts, packed)
-    keep, send = call(
-        functools.partial(rest_kernel, range(1, blocks)),
-        "correlate_rest",
-        jax.ShapeDtypeStruct((blocks, own, slab), F32),
-        jax.ShapeDtypeStruct((blocks, own, slab), F32),
-    )(hankel, scale, moves, own_terms, *library)
+    halves = jax.ShapeDtypeStruct((blocks - 1, own, slab), F32)
+    keep, send = call(functools.partial(early_kernel, distances[1:-1]), "correlate_early", halves, halves)(
+        hankel, scale, moves, own_terms, *library[:-1]
+    )
+    halves = jax.ShapeDtypeStruct((blocks, own, slab), F32)
+    keep, send = call(functools.partial(last_kernel, distances[-1]), "correlate_last", halves, halves)(
+        hankel, scale, moves, keep, send, library[-1]
+    )
     arrived = exchange(send, "sta", 1)
     piece = jax.ShapeDtypeStruct((own, slab), F32)
-    chips = call(assemble_kernel, "add_cores", *[piece] * blocks)(keep, arrived)
+    chips = call(functools.partial(assemble_kernel, distances), "add_cores", *[piece] * blocks)(keep, arrived)
     others = [exchange(chips[d], "sta", 2 * d) for d in range(blocks - 1, 0, -1)]
     stacked = chips[0]
     for part in others:

time: 28.4 us -> 26.4 us (0.930)
  Pallas kernels: 4.04 us -> 2.75 us
  waiting for transfers between devices: 11.9 us -> 10.7 us
    pallas_call x3 -> x5, Pallas kernels: 2.91 us -> 1.6 us  [the longest x1 0.7 us: per_device(): call(functools.partial(early_kernel, distances[1:-1]), 'correlate_early',...]
    ppermute x7, waiting for transfers between devices: 7.47 us -> 6.38 us  [exchange(): lax.ppermute(block, axis, [(i, i ^ distance) for i in range(lax.axis_size...]
    unnamed x6 -> x8, local copies, waits for them, and re-layouts: 0.91 us -> 0.92 us
  transfers between devices with their start and end apart: 8 -> 8, of which waited for: 6 -> 6; matrix products, arithmetic and copies ran while one was open for 0% -> 0% of each run, Pallas kernels for 4% -> 7%
where the time goes in v4:
time: 26.4 us; the launch traced here: 26 us
  starting transfers between devices  10.9 us (41%)
  waiting for transfers between devices  10.7 us (41%)
  Pallas kernels  2.75 us (10%)
  local copies, waits for them, and re-layouts  0.92 us (3%)
  other arithmetic  0.65 us (2%)
    ppermute x7, starting transfers between devices, exchange(): lax.ppermute(block, axis, [(i, i ^ distance) for i in range(lax.axis_size...  9.58 us
    ppermute x7, waiting for transfers between devices, exchange(): lax.ppermute(block, axis, [(i, i ^ distance) for i in range(lax.axis_size...  6.38 us
    ppermute x1, waiting for transfers between devices, per_device(): lax.ppermute(records[0], 'tm', [(i, i - 1) for i in range(1, blocks)])  4.33 us
    ppermute x1, starting transfers between devices, per_device(): lax.ppermute(records[0], 'tm', [(i, i - 1) for i in range(1, blocks)])  1.28 us
    pallas_call x1, Pallas kernels, per_device(): call(own_kernel, 'correlate_own', jax.ShapeDtypeStruct((3, TAPS_PAD, reac...  1.15 us
    unnamed x8, local copies, waits for them, and re-layouts  0.92 us
    pallas_call x1, Pallas kernels, per_device(): call(functools.partial(early_kernel, distances[1:-1]), 'correlate_early',...  0.7 us
    add x1, other arithmetic, per_device(): stacked = stacked + part  0.65 us
  transfers between devices with their start and end apart: 8, of which 6 were waited for; matrix products, arithmetic and copies ran while one was open for 0% of the time, Pallas kernels for 7%

profile of v4, /device:TPU:0, one launch (start us, length us, event | category | flops | bytes accessed | tf_op | source)
XLA Modules:
  0.0 26.0 jit_solution(12483482190572682612)
XLA Ops:
  0.0 0.0 copy-start.2
  0.0 0.0 copy-start
  0.0 0.0 copy-start.1
  0.0 0.0 copy-start.3
  0.0 0.7 %copy-done.2 = s32[1,3,64]{2,0,1:T(1,128)S(1)} copy-done((s32[1,3,64]{2,0,1:T(1,128)S(1)}, s32[1,3,64]{2,0,1:T(1,128)}, u32[]{:S(2)}) %copy-start.2) | copy-done | bytes 792
  0.7 0.2 copy-done
  0.9 0.3 %shape_templates.1.packed_ref = bf16[480,128]{1,0:T(8,128)(2,1)S(1)} custom-call(f32[64,64]{1,0:T(8,128)S(1)} %table.1.table_ref, bf16[3,64,300]{2,1,0:T(8,128)(2,1)S(1)} %bitcast.3, s32[3,1,64]{2,1,0:T(1,128)S(1)} %bitcast.6), custom_call_target="tpu_custom_call" | custom-call | flops 1000 | tf_op jit(solution)/shard_map/shape_templates/pallas_call | solution.py:179
  1.2 4.1 %collective-permute-start.2 = (bf16[480,128]{1,0:T(8,128)(2,1)S(1)}, bf16[480,128]{1,0:T(8,128)(2,1)S(1)}, u32[]{:S(2)}, u32[]{:S(2)}) collective-permute-start(bf16[480,128]{1,0:T(8,128)(2,1)S(1)} %shape_templates.1.packed_ref), channel_id=1, source_target_pairs={{0,2},{1,3},{2,0},{3,1},{4,6},{5,7},{6,4},{7,5},{8,10},{9,11},{10,... | collective-permute-start | bytes 368648 | tf_op jit(solution)/shard_map/ppermute | solution.py:162
  5.3 1.6 %collective-permute-start.1 = (bf16[480,128]{1,0:T(8,128)(2,1)S(1)}, bf16[480,128]{1,0:T(8,128)(2,1)S(1)}, u32[]{:S(2)}, u32[]{:S(2)}) collective-permute-start(bf16[480,128]{1,0:T(8,128)(2,1)S(1)} %shape_templates.1.packed_ref), channel_id=1, source_target_pairs={{0,1},{1,0},{2,3},{3,2},{4,5},{5,4},{6,7},{7,6},{8,9},{9,8},{10,11... | collective-permute-start | bytes 368648 | tf_op jit(solution)/shard_map/ppermute | solution.py:162
  6.9 0.0 collective-permute-start.3
  6.9 0.0 copy-done.1
  6.9 1.3 %collective-permute-start = (bf16[3,512]{1,0:T(4,128)(2,1)S(1)}, bf16[3,512]{1,0:T(4,128)(2,1)S(1)}, u32[]{:S(2)}, u32[]{:S(2)}) collective-permute-start(bf16[3,512]{1,0:T(4,128)(2,1)S(1)} %bitcast.4), channel_id=1, source_target_pairs={{1,0},{2,1},{3,2},{5,4},{6,5},{7,6},{9,8},{10,9},{11,10},{13,12},{... | collective-permute-start | bytes 9224 | tf_op jit(solution)/shard_map/ppermute | solution.py:184
  8.2 4.3 %collective-permute-done.following_ref = bf16[3,512]{1,0:T(4,128)(2,1)S(1)} collective-permute-done((bf16[3,512]{1,0:T(4,128)(2,1)S(1)}, bf16[3,512]{1,0:T(4,128)(2,1)S(1)}, u32[]{:S(2)}, u32[]{:S(2)}) %collective-permute-start) | collective-permute-done | bytes 3104 | tf_op jit(solution)/shard_map/ppermute | solution.py:184
  12.5 0.0 copy-done.3
  12.5 1.2 %correlate_own.1 = (bf16[3,384,768]{2,1,0:T(8,128)(2,1)S(1)}, f32[3,768]{1,0:T(4,128)S(1)}, s32[1,256]{1,0:T(1,128)S(1)}, f32[64,512]{1,0:T(8,128)S(1)}) custom-call(bf16[3,512]{1,0:T(4,128)(2,1)S(1)} %bitcast.5, bf16[3,512]{1,0:T(4,128)(2,1)S(1)} %collective-permute-done.following_ref, s32[1,256]{1,0:T(1,128)S(1)} %copy-done.3, ...), custom_call_target="tpu_custom_call" | custom-call | flops 1000 | tf_op jit(solution)/shard_map/correlate_own/pallas_call | solution.py:185
  13.7 0.0 collective-permute-done.2.refs_1_
  13.7 0.0 collective-permute-done.1.refs_0_
  13.7 0.7 %correlate_early.1 = (f32[3,32,512]{2,1,0:T(8,128)S(1)}, f32[3,32,512]{2,1,0:T(8,128)S(1)}) custom-call(bf16[3,384,768]{2,1,0:T(8,128)(2,1)S(1)} %get-tuple-element.17.hankel_ref, f32[3,768]{1,0:T(4,128)S(1)} %get-tuple-element.18.scale_ref, s32[1,256]{1,0:T(1,128)S(1)} %get-tuple-element.19.moves_ref, f32[64,512]{1,0:T(8,128)S(1)} %get-tuple-element.20.own_ref, ...), custom_call_target="tpu_custom_call" | custom-call | flops 1000 | tf_op jit(solution)/shard_map/correlate_early/pallas_call | solution.py:194
  14.4 0.7 %collective-permute-done.3.packed_ref = bf16[480,128]{1,0:T(8,128)(2,1)S(1)} collective-permute-done((bf16[480,128]{1,0:T(8,128)(2,1)S(1)}, bf16[480,128]{1,0:T(8,128)(2,1)S(1)}, u32[]{:S(2)}, u32[]{:S(2)}) %collective-permute-start.3) | collective-permute-done | bytes 122912 | tf_op jit(solution)/shard_map/ppermute | solution.py:162
  15.1 0.5 %correlate_last.1 = (f32[4,32,512]{2,1,0:T(8,128)S(1)}, f32[4,32,512]{2,1,0:T(8,128)S(1)}) custom-call(bf16[3,384,768]{2,1,0:T(8,128)(2,1)S(1)} %get-tuple-element.17.hankel_ref, f32[3,768]{1,0:T(4,128)S(1)} %get-tuple-element.18.scale_ref, s32[1,256]{1,0:T(1,128)S(1)} %get-tuple-element.19.moves_ref, f32[3,32,512]{2,1,0:T(8,128)S(1)} %get-tuple-element.21.early_keep_ref, ...), custom_call_target="tpu_custom_call" | custom-call | flops 1000 | tf_op jit(solution)/shard_map/correlate_last/pallas_call | solution.py:198
  15.6 0.1 collective-permute-start.4
  15.7 1.5 %collective-permute-done.4.arrived_ref = f32[4,32,512]{2,1,0:T(8,128)S(1)} collective-permute-done((f32[4,32,512]{2,1,0:T(8,128)S(1)}, f32[4,32,512]{2,1,0:T(8,128)S(1)}, u32[]{:S(2)}, u32[]{:S(2)}) %collective-permute-start.4) | collective-permute-done | bytes 262176 | tf_op jit(solution)/shard_map/ppermute | solution.py:162
  17.2 0.1 add_cores.1
  17.3 3.2 %collective-permute-start.5 = (f32[32,512]{1,0:T(8,128)S(1)}, f32[32,512]{1,0:T(8,128)S(1)}, u32[]{:S(2)}, u32[]{:S(2)}) collective-permute-start(f32[32,512]{1,0:T(8,128)S(1)} %get-tuple-element.26), channel_id=1, source_target_pairs={{0,24},{4,28},{8,16},{12,20},{16,8},{20,12},{24,0},{28,4},{1,25},{... | collective-permute-start | bytes 196616 | tf_op jit(solution)/shard_map/ppermute | solution.py:162
  20.5 0.5 %collective-permute-start.6 = (f32[32,512]{1,0:T(8,128)S(1)}, f32[32,512]{1,0:T(8,128)S(1)}, u32[]{:S(2)}, u32[]{:S(2)}) collective-permute-start(f32[32,512]{1,0:T(8,128)S(1)} %get-tuple-element.27), channel_id=1, source_target_pairs={{0,16},{4,20},{8,24},{12,28},{16,0},{20,4},{24,8},{28,12},{1,17},{... | collective-permute-start | bytes 196616 | tf_op jit(solution)/shard_map/ppermute | solution.py:162
  21.0 0.1 collective-permute-start.7
  21.2 1.8 %collective-permute-done.5 = f32[32,512]{1,0:T(8,128)S(1)} collective-permute-done((f32[32,512]{1,0:T(8,128)S(1)}, f32[32,512]{1,0:T(8,128)S(1)}, u32[]{:S(2)}, u32[]{:S(2)}) %collective-permute-start.5) | collective-permute-done | bytes 65568 | tf_op jit(solution)/shard_map/ppermute | solution.py:162
  22.9 1.9 %collective-permute-done.6 = f32[32,512]{1,0:T(8,128)S(1)} collective-permute-done((f32[32,512]{1,0:T(8,128)S(1)}, f32[32,512]{1,0:T(8,128)S(1)}, u32[]{:S(2)}, u32[]{:S(2)}) %collective-permute-start.6) | collective-permute-done | bytes 65568 | tf_op jit(solution)/shard_map/ppermute | solution.py:162
  24.8 0.5 %collective-permute-done.7 = f32[32,512]{1,0:T(8,128)S(1)} collective-permute-done((f32[32,512]{1,0:T(8,128)S(1)}, f32[32,512]{1,0:T(8,128)S(1)}, u32[]{:S(2)}, u32[]{:S(2)}) %collective-permute-start.7) | collective-permute-done | bytes 65568 | tf_op jit(solution)/shard_map/ppermute | solution.py:162
  25.3 0.6 %add_add_fusion = f32[32,512]{1,0:T(8,128)} fusion(f32[32,512]{1,0:T(8,128)S(1)} %collective-permute-done.7, f32[32,512]{1,0:T(8,128)S(1)} %collective-permute-done.6, f32[32,512]{1,0:T(8,128)S(1)} %get-tuple-element.25, f32[32,512]{1,0:T(8,128)S(1)} %collective-permute-done.5), kind=kLoop, calls=%fused_computation | loop fusion | flops 49152 | bytes 327680 | tf_op jit(solution)/shard_map/add | solution.py:207
  (1 shorter events, 0.0 us)
Async XLA Ops:
  0.0 0.7 %copy-start.2 = (s32[1,3,64]{2,0,1:T(1,128)S(1)}, s32[1,3,64]{2,0,1:T(1,128)}, u32[]{:S(2)}) copy-start(s32[1,3,64]{2,0,1:T(1,128)} %param.6) | copy-start | bytes 2308
  0.0 0.9 %copy-start = (bf16[1,3,64,300]{3,2,1,0:T(8,128)(2,1)S(1)}, bf16[1,3,64,300]{3,2,1,0:T(8,128)(2,1)}, u32[]{:S(2)}) copy-start(bf16[1,3,64,300]{3,2,1,0:T(8,128)(2,1)} %param.5) | copy-start | bytes 345604
  0.0 6.9 %copy-start.1 = (bf16[1,3,512]{2,1,0:T(4,128)(2,1)S(1)}, bf16[1,3,512]{2,1,0:T(4,128)(2,1)}, u32[]{:S(2)}) copy-start(bf16[1,3,512]{2,1,0:T(4,128)(2,1)} %param.4) | copy-start | bytes 9220
  0.0 12.5 %copy-start.3 = (s32[1,256]{1,0:T(1,128)S(1)}, s32[1,256]{1,0:T(1,128)}, u32[]{:S(2)}) copy-start(s32[1,256]{1,0:T(1,128)} %moves_ref.1) | copy-start | bytes 3076
  1.2 12.5 %collective-permute-start.2 = (bf16[480,128]{1,0:T(8,128)(2,1)S(1)}, bf16[480,128]{1,0:T(8,128)(2,1)S(1)}, u32[]{:S(2)}, u32[]{:S(2)}) collective-permute-start(bf16[480,128]{1,0:T(8,128)(2,1)S(1)} %shape_templates.1.packed_ref), channel_id=1, source_target_pairs={{0,2},{1,3},{2,0},{3,1},{4,6},{5,7},{6,4},{7,5},{8,10},{9,11},{10,... | collective-permute-start | bytes 368648 | tf_op jit(solution)/shard_map/ppermute | solution.py:162
  5.3 8.4 %collective-permute-start.1 = (bf16[480,128]{1,0:T(8,128)(2,1)S(1)}, bf16[480,128]{1,0:T(8,128)(2,1)S(1)}, u32[]{:S(2)}, u32[]{:S(2)}) collective-permute-start(bf16[480,128]{1,0:T(8,128)(2,1)S(1)} %shape_templates.1.packed_ref), channel_id=1, source_target_pairs={{0,1},{1,0},{2,3},{3,2},{4,5},{5,4},{6,7},{7,6},{8,9},{9,8},{10,11... | collective-permute-start | bytes 368648 | tf_op jit(solution)/shard_map/ppermute | solution.py:162
  6.9 8.2 %collective-permute-start.3 = (bf16[480,128]{1,0:T(8,128)(2,1)S(1)}, bf16[480,128]{1,0:T(8,128)(2,1)S(1)}, u32[]{:S(2)}, u32[]{:S(2)}) collective-permute-start(bf16[480,128]{1,0:T(8,128)(2,1)S(1)} %shape_templates.1.packed_ref), channel_id=1, source_target_pairs={{0,3},{1,2},{2,1},{3,0},{4,7},{5,6},{6,5},{7,4},{8,11},{9,10},{10,... | collective-permute-start | bytes 368648 | tf_op jit(solution)/shard_map/ppermute | solution.py:162
  6.9 5.6 %collective-permute-start = (bf16[3,512]{1,0:T(4,128)(2,1)S(1)}, bf16[3,512]{1,0:T(4,128)(2,1)S(1)}, u32[]{:S(2)}, u32[]{:S(2)}) collective-permute-start(bf16[3,512]{1,0:T(4,128)(2,1)S(1)} %bitcast.4), channel_id=1, source_target_pairs={{1,0},{2,1},{3,2},{5,4},{6,5},{7,6},{9,8},{10,9},{11,10},{13,12},{... | collective-permute-start | bytes 9224 | tf_op jit(solution)/shard_map/ppermute | solution.py:184
  15.6 1.6 %collective-permute-start.4 = (f32[4,32,512]{2,1,0:T(8,128)S(1)}, f32[4,32,512]{2,1,0:T(8,128)S(1)}, u32[]{:S(2)}, u32[]{:S(2)}) collective-permute-start(f32[4,32,512]{2,1,0:T(8,128)S(1)} %get-tuple-element.24), channel_id=1, source_target_pairs={{0,4},{4,0},{8,12},{12,8},{16,20},{20,16},{24,28},{28,24},{1,5},{5... | collective-permute-start | bytes 786440 | tf_op jit(solution)/shard_map/ppermute | solution.py:162
  17.3 5.6 %collective-permute-start.5 = (f32[32,512]{1,0:T(8,128)S(1)}, f32[32,512]{1,0:T(8,128)S(1)}, u32[]{:S(2)}, u32[]{:S(2)}) collective-permute-start(f32[32,512]{1,0:T(8,128)S(1)} %get-tuple-element.26), channel_id=1, source_target_pairs={{0,24},{4,28},{8,16},{12,20},{16,8},{20,12},{24,0},{28,4},{1,25},{... | collective-permute-start | bytes 196616 | tf_op jit(solution)/shard_map/ppermute | solution.py:162
  20.5 4.3 %collective-permute-start.6 = (f32[32,512]{1,0:T(8,128)S(1)}, f32[32,512]{1,0:T(8,128)S(1)}, u32[]{:S(2)}, u32[]{:S(2)}) collective-permute-start(f32[32,512]{1,0:T(8,128)S(1)} %get-tuple-element.27), channel_id=1, source_target_pairs={{0,16},{4,20},{8,24},{12,28},{16,0},{20,4},{24,8},{28,12},{1,17},{... | collective-permute-start | bytes 196616 | tf_op jit(solution)/shard_map/ppermute | solution.py:162
  21.0 4.3 %collective-permute-start.7 = (f32[32,512]{1,0:T(8,128)S(1)}, f32[32,512]{1,0:T(8,128)S(1)}, u32[]{:S(2)}, u32[]{:S(2)}) collective-permute-start(f32[32,512]{1,0:T(8,128)S(1)} %get-tuple-element.28), channel_id=1, source_target_pairs={{0,8},{4,12},{8,0},{12,4},{16,24},{20,28},{24,16},{28,20},{1,9},{5... | collective-permute-start | bytes 196616 | tf_op jit(solution)/shard_map/ppermute | solution.py:162

commit v5 on v4

--- a/solution.py
+++ b/solution.py
@@ -12,7 +12,7 @@
 F32 = jnp.float32
 BF16 = jnp.bfloat16
 SMALL = pltpu.CompilerParams(vmem_limit_bytes=16 << 20)
-COST = {"table": 10**10}
+COST = {"table": 10**10, "correlate_own": 10**9, "correlate_early": 10**9}
 
 
 def column_of(row, rows, first):

time: 26.4 us -> 25.5 us (0.966); the launches traced: 26 us -> 25.4 us
  waiting for transfers between devices: 10.7 us -> 7.91 us
  starting transfers between devices: 10.9 us -> 13.1 us
    ppermute x1, waiting for transfers between devices: 4.33 us -> 1.77 us  [per_device(): lax.ppermute(records[0], 'tm', [(i, i - 1) for i in range(1, blocks)])]
    ppermute x7, starting transfers between devices: 9.58 us -> 11.8 us  [exchange(): lax.ppermute(block, axis, [(i, i ^ distance) for i in range(lax.axis_size...]
where the time goes in v5:
time: 25.5 us; the launch traced here: 25.4 us
  starting transfers between devices  13.1 us (51%)
  waiting for transfers between devices  7.91 us (31%)
  Pallas kernels  2.75 us (11%)
  local copies, waits for them, and re-layouts  0.92 us (4%)
  other arithmetic  0.65 us (3%)
    ppermute x7, starting transfers between devices, exchange(): lax.ppermute(block, axis, [(i, i ^ distance) for i in range(lax.axis_size...  11.8 us
    ppermute x7, waiting for transfers between devices, exchange(): lax.ppermute(block, axis, [(i, i ^ distance) for i in range(lax.axis_size...  6.15 us
    ppermute x1, waiting for transfers between devices, per_device(): lax.ppermute(records[0], 'tm', [(i, i - 1) for i in range(1, blocks)])  1.77 us
    ppermute x1, starting transfers between devices, per_device(): lax.ppermute(records[0], 'tm', [(i, i - 1) for i in range(1, blocks)])  1.28 us
    pallas_call x1, Pallas kernels, per_device(): call(own_kernel, 'correlate_own', jax.ShapeDtypeStruct((3, TAPS_PAD, reac...  1.15 us
    unnamed x8, local copies, waits for them, and re-layouts  0.92 us
    pallas_call x1, Pallas kernels, per_device(): call(functools.partial(early_kernel, distances[1:-1]), 'correlate_early',...  0.7 us
    add x1, other arithmetic, per_device(): stacked = stacked + part  0.65 us
  transfers between devices with their start and end apart: 8, of which 6 were waited for; matrix products, arithmetic and copies ran while one was open for 0% of the time, Pallas kernels for 7%

profile of v5, /device:TPU:0, one launch (start us, length us, event | category | flops | bytes accessed | tf_op | source)
XLA Modules:
  0.0 25.4 jit_solution(9579599026064245002)
XLA Ops:
  0.0 0.0 copy-start.1
  0.0 0.0 copy-start
  0.0 0.0 copy-start.2
  0.0 0.0 copy-start.3
  0.0 0.7 %copy-done.1 = s32[1,3,64]{2,0,1:T(1,128)S(1)} copy-done((s32[1,3,64]{2,0,1:T(1,128)S(1)}, s32[1,3,64]{2,0,1:T(1,128)}, u32[]{:S(2)}) %copy-start.1) | copy-done | bytes 792
  0.7 0.2 copy-done
  0.9 0.3 %shape_templates.1.packed_ref = bf16[480,128]{1,0:T(8,128)(2,1)S(1)} custom-call(f32[64,64]{1,0:T(8,128)S(1)} %table.1.table_ref, bf16[3,64,300]{2,1,0:T(8,128)(2,1)S(1)} %bitcast.3, s32[3,1,64]{2,1,0:T(1,128)S(1)} %bitcast.4), custom_call_target="tpu_custom_call" | custom-call | flops 1000 | tf_op jit(solution)/shard_map/shape_templates/pallas_call | solution.py:179
  1.2 4.1 %collective-permute-start.2 = (bf16[480,128]{1,0:T(8,128)(2,1)S(1)}, bf16[480,128]{1,0:T(8,128)(2,1)S(1)}, u32[]{:S(2)}, u32[]{:S(2)}) collective-permute-start(bf16[480,128]{1,0:T(8,128)(2,1)S(1)} %shape_templates.1.packed_ref), channel_id=1, source_target_pairs={{0,2},{1,3},{2,0},{3,1},{4,6},{5,7},{6,4},{7,5},{8,10},{9,11},{10,... | collective-permute-start | bytes 368648 | tf_op jit(solution)/shard_map/ppermute | solution.py:162
  5.3 1.6 %collective-permute-start.1 = (bf16[480,128]{1,0:T(8,128)(2,1)S(1)}, bf16[480,128]{1,0:T(8,128)(2,1)S(1)}, u32[]{:S(2)}, u32[]{:S(2)}) collective-permute-start(bf16[480,128]{1,0:T(8,128)(2,1)S(1)} %shape_templates.1.packed_ref), channel_id=1, source_target_pairs={{0,1},{1,0},{2,3},{3,2},{4,5},{5,4},{6,7},{7,6},{8,9},{9,8},{10,11... | collective-permute-start | bytes 368648 | tf_op jit(solution)/shard_map/ppermute | solution.py:162
  6.9 0.0 copy-done.2
  6.9 1.3 %collective-permute-start = (bf16[3,512]{1,0:T(4,128)(2,1)S(1)}, bf16[3,512]{1,0:T(4,128)(2,1)S(1)}, u32[]{:S(2)}, u32[]{:S(2)}) collective-permute-start(bf16[3,512]{1,0:T(4,128)(2,1)S(1)} %bitcast.5), channel_id=1, source_target_pairs={{1,0},{2,1},{3,2},{5,4},{6,5},{7,6},{9,8},{10,9},{11,10},{13,12},{... | collective-permute-start | bytes 9224 | tf_op jit(solution)/shard_map/ppermute | solution.py:184
  8.2 2.5 %collective-permute-start.3 = (bf16[480,128]{1,0:T(8,128)(2,1)S(1)}, bf16[480,128]{1,0:T(8,128)(2,1)S(1)}, u32[]{:S(2)}, u32[]{:S(2)}) collective-permute-start(bf16[480,128]{1,0:T(8,128)(2,1)S(1)} %shape_templates.1.packed_ref), channel_id=1, source_target_pairs={{0,3},{1,2},{2,1},{3,0},{4,7},{5,6},{6,5},{7,4},{8,11},{9,10},{10,... | collective-permute-start | bytes 368648 | tf_op jit(solution)/shard_map/ppermute | solution.py:162
  10.6 1.8 %collective-permute-done.following_ref = bf16[3,512]{1,0:T(4,128)(2,1)S(1)} collective-permute-done((bf16[3,512]{1,0:T(4,128)(2,1)S(1)}, bf16[3,512]{1,0:T(4,128)(2,1)S(1)}, u32[]{:S(2)}, u32[]{:S(2)}) %collective-permute-start) | collective-permute-done | bytes 3104 | tf_op jit(solution)/shard_map/ppermute | solution.py:184
  12.4 0.0 copy-done.3
  12.4 1.1 %correlate_own.1 = (bf16[3,384,768]{2,1,0:T(8,128)(2,1)S(1)}, f32[3,768]{1,0:T(4,128)S(1)}, s32[1,256]{1,0:T(1,128)S(1)}, f32[64,512]{1,0:T(8,128)S(1)}) custom-call(bf16[3,512]{1,0:T(4,128)(2,1)S(1)} %bitcast.6, bf16[3,512]{1,0:T(4,128)(2,1)S(1)} %collective-permute-done.following_ref, s32[1,256]{1,0:T(1,128)S(1)} %copy-done.3, ...), custom_call_target="tpu_custom_call" | custom-call | flops 1000000000 | tf_op jit(solution)/shard_map/correlate_own/pallas_call | solution.py:185
  13.6 0.0 collective-permute-done.2.refs_1_
  13.6 0.0 collective-permute-done.1.refs_0_
  13.6 0.7 %correlate_early.1 = (f32[3,32,512]{2,1,0:T(8,128)S(1)}, f32[3,32,512]{2,1,0:T(8,128)S(1)}) custom-call(bf16[3,384,768]{2,1,0:T(8,128)(2,1)S(1)} %get-tuple-element.17.hankel_ref, f32[3,768]{1,0:T(4,128)S(1)} %get-tuple-element.18.scale_ref, s32[1,256]{1,0:T(1,128)S(1)} %get-tuple-element.19.moves_ref, f32[64,512]{1,0:T(8,128)S(1)} %get-tuple-element.20.own_ref, ...), custom_call_target="tpu_custom_call" | custom-call | flops 1000000000 | tf_op jit(solution)/shard_map/correlate_early/pallas_call | solution.py:194
  14.3 0.9 %collective-permute-done.3.packed_ref = bf16[480,128]{1,0:T(8,128)(2,1)S(1)} collective-permute-done((bf16[480,128]{1,0:T(8,128)(2,1)S(1)}, bf16[480,128]{1,0:T(8,128)(2,1)S(1)}, u32[]{:S(2)}, u32[]{:S(2)}) %collective-permute-start.3) | collective-permute-done | bytes 122912 | tf_op jit(solution)/shard_map/ppermute | solution.py:162
  15.2 0.5 %correlate_last.1 = (f32[4,32,512]{2,1,0:T(8,128)S(1)}, f32[4,32,512]{2,1,0:T(8,128)S(1)}) custom-call(bf16[3,384,768]{2,1,0:T(8,128)(2,1)S(1)} %get-tuple-element.17.hankel_ref, f32[3,768]{1,0:T(4,128)S(1)} %get-tuple-element.18.scale_ref, s32[1,256]{1,0:T(1,128)S(1)} %get-tuple-element.19.moves_ref, f32[3,32,512]{2,1,0:T(8,128)S(1)} %get-tuple-element.21.early_keep_ref, ...), custom_call_target="tpu_custom_call" | custom-call | flops 1000 | tf_op jit(solution)/shard_map/correlate_last/pallas_call | solution.py:198
  15.7 0.1 collective-permute-start.4
  15.8 1.5 %collective-permute-done.4.arrived_ref = f32[4,32,512]{2,1,0:T(8,128)S(1)} collective-permute-done((f32[4,32,512]{2,1,0:T(8,128)S(1)}, f32[4,32,512]{2,1,0:T(8,128)S(1)}, u32[]{:S(2)}, u32[]{:S(2)}) %collective-permute-start.4) | collective-permute-done | bytes 262176 | tf_op jit(solution)/shard_map/ppermute | solution.py:162
  17.3 0.1 add_cores.1
  17.4 2.5 %collective-permute-start.5 = (f32[32,512]{1,0:T(8,128)S(1)}, f32[32,512]{1,0:T(8,128)S(1)}, u32[]{:S(2)}, u32[]{:S(2)}) collective-permute-start(f32[32,512]{1,0:T(8,128)S(1)} %get-tuple-element.26), channel_id=1, source_target_pairs={{0,24},{4,28},{8,16},{12,20},{16,8},{20,12},{24,0},{28,4},{1,25},{... | collective-permute-start | bytes 196616 | tf_op jit(solution)/shard_map/ppermute | solution.py:162
  19.9 0.5 %collective-permute-start.6 = (f32[32,512]{1,0:T(8,128)S(1)}, f32[32,512]{1,0:T(8,128)S(1)}, u32[]{:S(2)}, u32[]{:S(2)}) collective-permute-start(f32[32,512]{1,0:T(8,128)S(1)} %get-tuple-element.27), channel_id=1, source_target_pairs={{0,16},{4,20},{8,24},{12,28},{16,0},{20,4},{24,8},{28,12},{1,17},{... | collective-permute-start | bytes 196616 | tf_op jit(solution)/shard_map/ppermute | solution.py:162
  20.4 0.5 %collective-permute-start.7 = (f32[32,512]{1,0:T(8,128)S(1)}, f32[32,512]{1,0:T(8,128)S(1)}, u32[]{:S(2)}, u32[]{:S(2)}) collective-permute-start(f32[32,512]{1,0:T(8,128)S(1)} %get-tuple-element.28), channel_id=1, source_target_pairs={{0,8},{4,12},{8,0},{12,4},{16,24},{20,28},{24,16},{28,20},{1,9},{5... | collective-permute-start | bytes 196616 | tf_op jit(solution)/shard_map/ppermute | solution.py:162
  21.0 1.7 %collective-permute-done.5 = f32[32,512]{1,0:T(8,128)S(1)} collective-permute-done((f32[32,512]{1,0:T(8,128)S(1)}, f32[32,512]{1,0:T(8,128)S(1)}, u32[]{:S(2)}, u32[]{:S(2)}) %collective-permute-start.5) | collective-permute-done | bytes 65568 | tf_op jit(solution)/shard_map/ppermute | solution.py:162
  22.7 1.5 %collective-permute-done.6 = f32[32,512]{1,0:T(8,128)S(1)} collective-permute-done((f32[32,512]{1,0:T(8,128)S(1)}, f32[32,512]{1,0:T(8,128)S(1)}, u32[]{:S(2)}, u32[]{:S(2)}) %collective-permute-start.6) | collective-permute-done | bytes 65568 | tf_op jit(solution)/shard_map/ppermute | solution.py:162
  24.2 0.5 %collective-permute-done.7 = f32[32,512]{1,0:T(8,128)S(1)} collective-permute-done((f32[32,512]{1,0:T(8,128)S(1)}, f32[32,512]{1,0:T(8,128)S(1)}, u32[]{:S(2)}, u32[]{:S(2)}) %collective-permute-start.7) | collective-permute-done | bytes 65568 | tf_op jit(solution)/shard_map/ppermute | solution.py:162
  24.7 0.6 %add_add_fusion = f32[32,512]{1,0:T(8,128)} fusion(f32[32,512]{1,0:T(8,128)S(1)} %collective-permute-done.7, f32[32,512]{1,0:T(8,128)S(1)} %collective-permute-done.6, f32[32,512]{1,0:T(8,128)S(1)} %get-tuple-element.25, f32[32,512]{1,0:T(8,128)S(1)} %collective-permute-done.5), kind=kLoop, calls=%fused_computation | loop fusion | flops 49152 | bytes 327680 | tf_op jit(solution)/shard_map/add | solution.py:207
  (1 shorter events, 0.0 us)
Async XLA Ops:
  0.0 0.7 %copy-start.1 = (s32[1,3,64]{2,0,1:T(1,128)S(1)}, s32[1,3,64]{2,0,1:T(1,128)}, u32[]{:S(2)}) copy-start(s32[1,3,64]{2,0,1:T(1,128)} %param.6) | copy-start | bytes 2308
  0.0 0.9 %copy-start = (bf16[1,3,64,300]{3,2,1,0:T(8,128)(2,1)S(1)}, bf16[1,3,64,300]{3,2,1,0:T(8,128)(2,1)}, u32[]{:S(2)}) copy-start(bf16[1,3,64,300]{3,2,1,0:T(8,128)(2,1)} %param.5) | copy-start | bytes 345604
  0.0 6.9 %copy-start.2 = (bf16[1,3,512]{2,1,0:T(4,128)(2,1)S(1)}, bf16[1,3,512]{2,1,0:T(4,128)(2,1)}, u32[]{:S(2)}) copy-start(bf16[1,3,512]{2,1,0:T(4,128)(2,1)} %param.4) | copy-start | bytes 9220
  0.0 12.4 %copy-start.3 = (s32[1,256]{1,0:T(1,128)S(1)}, s32[1,256]{1,0:T(1,128)}, u32[]{:S(2)}) copy-start(s32[1,256]{1,0:T(1,128)} %moves_ref.1) | copy-start | bytes 3076
  1.2 12.4 %collective-permute-start.2 = (bf16[480,128]{1,0:T(8,128)(2,1)S(1)}, bf16[480,128]{1,0:T(8,128)(2,1)S(1)}, u32[]{:S(2)}, u32[]{:S(2)}) collective-permute-start(bf16[480,128]{1,0:T(8,128)(2,1)S(1)} %shape_templates.1.packed_ref), channel_id=1, source_target_pairs={{0,2},{1,3},{2,0},{3,1},{4,6},{5,7},{6,4},{7,5},{8,10},{9,11},{10,... | collective-permute-start | bytes 368648 | tf_op jit(solution)/shard_map/ppermute | solution.py:162
  5.3 8.3 %collective-permute-start.1 = (bf16[480,128]{1,0:T(8,128)(2,1)S(1)}, bf16[480,128]{1,0:T(8,128)(2,1)S(1)}, u32[]{:S(2)}, u32[]{:S(2)}) collective-permute-start(bf16[480,128]{1,0:T(8,128)(2,1)S(1)} %shape_templates.1.packed_ref), channel_id=1, source_target_pairs={{0,1},{1,0},{2,3},{3,2},{4,5},{5,4},{6,7},{7,6},{8,9},{9,8},{10,11... | collective-permute-start | bytes 368648 | tf_op jit(solution)/shard_map/ppermute | solution.py:162
  6.9 5.5 %collective-permute-start = (bf16[3,512]{1,0:T(4,128)(2,1)S(1)}, bf16[3,512]{1,0:T(4,128)(2,1)S(1)}, u32[]{:S(2)}, u32[]{:S(2)}) collective-permute-start(bf16[3,512]{1,0:T(4,128)(2,1)S(1)} %bitcast.5), channel_id=1, source_target_pairs={{1,0},{2,1},{3,2},{5,4},{6,5},{7,6},{9,8},{10,9},{11,10},{13,12},{... | collective-permute-start | bytes 9224 | tf_op jit(solution)/shard_map/ppermute | solution.py:184
  8.2 7.0 %collective-permute-start.3 = (bf16[480,128]{1,0:T(8,128)(2,1)S(1)}, bf16[480,128]{1,0:T(8,128)(2,1)S(1)}, u32[]{:S(2)}, u32[]{:S(2)}) collective-permute-start(bf16[480,128]{1,0:T(8,128)(2,1)S(1)} %shape_templates.1.packed_ref), channel_id=1, source_target_pairs={{0,3},{1,2},{2,1},{3,0},{4,7},{5,6},{6,5},{7,4},{8,11},{9,10},{10,... | collective-permute-start | bytes 368648 | tf_op jit(solution)/shard_map/ppermute | solution.py:162
  15.7 1.6 %collective-permute-start.4 = (f32[4,32,512]{2,1,0:T(8,128)S(1)}, f32[4,32,512]{2,1,0:T(8,128)S(1)}, u32[]{:S(2)}, u32[]{:S(2)}) collective-permute-start(f32[4,32,512]{2,1,0:T(8,128)S(1)} %get-tuple-element.24), channel_id=1, source_target_pairs={{0,4},{4,0},{8,12},{12,8},{16,20},{20,16},{24,28},{28,24},{1,5},{5... | collective-permute-start | bytes 786440 | tf_op jit(solution)/shard_map/ppermute | solution.py:162
  17.4 5.3 %collective-permute-start.5 = (f32[32,512]{1,0:T(8,128)S(1)}, f32[32,512]{1,0:T(8,128)S(1)}, u32[]{:S(2)}, u32[]{:S(2)}) collective-permute-start(f32[32,512]{1,0:T(8,128)S(1)} %get-tuple-element.26), channel_id=1, source_target_pairs={{0,24},{4,28},{8,16},{12,20},{16,8},{20,12},{24,0},{28,4},{1,25},{... | collective-permute-start | bytes 196616 | tf_op jit(solution)/shard_map/ppermute | solution.py:162
  19.9 4.3 %collective-permute-start.6 = (f32[32,512]{1,0:T(8,128)S(1)}, f32[32,512]{1,0:T(8,128)S(1)}, u32[]{:S(2)}, u32[]{:S(2)}) collective-permute-start(f32[32,512]{1,0:T(8,128)S(1)} %get-tuple-element.27), channel_id=1, source_target_pairs={{0,16},{4,20},{8,24},{12,28},{16,0},{20,4},{24,8},{28,12},{1,17},{... | collective-permute-start | bytes 196616 | tf_op jit(solution)/shard_map/ppermute | solution.py:162
  20.4 4.3 %collective-permute-start.7 = (f32[32,512]{1,0:T(8,128)S(1)}, f32[32,512]{1,0:T(8,128)S(1)}, u32[]{:S(2)}, u32[]{:S(2)}) collective-permute-start(f32[32,512]{1,0:T(8,128)S(1)} %get-tuple-element.28), channel_id=1, source_target_pairs={{0,8},{4,12},{8,0},{12,4},{16,24},{20,28},{24,16},{28,20},{1,9},{5... | collective-permute-start | bytes 196616 | tf_op jit(solution)/shard_map/ppermute | solution.py:162

commit v6 on v5

--- a/solution.py
+++ b/solution.py
@@ -60,7 +60,9 @@
     reach = hankel_ref.shape[2]
     sub = lax.broadcasted_iota(jnp.int32, (8, length), 0)
     for c in range(3):
-        row = jnp.concatenate([slab_ref[c : c + 1, :], following_ref[c : c + 1, :]], axis=1).astype(F32)
+        later = following_ref[c : c + 1, :].astype(F32)
+        later = jnp.where(lax.axis_index("tm") == lax.axis_size("tm") - 1, 0.0, later)
+        row = jnp.concatenate([slab_ref[c : c + 1, :].astype(F32), later], axis=1)
         stair = jnp.broadcast_to(row, (8, length))
         for bit in (1, 2, 4):
             stair = jnp.where((sub & bit) != 0, pltpu.roll(stair, length - bit, 1), stair)
@@ -139,18 +141,21 @@
     store_halves([own_ref[...]] + results, keep_ref, send_ref, 0)
 
 
-def last_kernel(distance, hankel_ref, scale_ref, moves_ref, early_keep_ref, early_send_ref, packed_ref, keep_ref, send_ref):
-    early = early_keep_ref.shape[0]
-    keep_ref[0:early] = early_keep_ref[...]
+def last_kernel(distance, hankel_ref, scale_ref, moves_ref, early_send_ref, packed_ref, keep_ref, send_ref):
+    early = early_send_ref.shape[0]
     send_ref[0:early] = early_send_ref[...]
-    results = correlate([packed_ref], [distance], hankel_ref, scale_ref, moves_ref, keep_ref.shape[2])
-    store_halves(results, keep_ref, send_ref, early)
-
-
-def assemble_kernel(distances, keep_ref, arrived_ref, *out_refs):
+    (result,) = correlate([packed_ref], [distance], hankel_ref, scale_ref, moves_ref, keep_ref.shape[2])
+    own = keep_ref.shape[1]
+    odd = lax.axis_index("sta") % 2 == 1
+    keep_ref[0] = jnp.where(odd, result[own:], result[:own])
+    send_ref[early] = jnp.where(odd, result[:own], result[own:])
+
+
+def assemble_kernel(distances, keep_ref, last_keep_ref, arrived_ref, *out_refs):
     chip = lax.axis_index("sta") // 2
     for i, distance in enumerate(distances):
-        value = keep_ref[i] + arrived_ref[i]
+        kept = keep_ref[i] if i < keep_ref.shape[0] else last_keep_ref[0]
+        value = kept + arrived_ref[i]
         for j, out_ref in enumerate(out_refs):
 
             @pl.when(chip ^ lax.axis_index("tm") ^ distance == j)
@@ -181,7 +186,7 @@
     )
     distances = list(range(blocks))
     library = [exchange(packed, "tm", i) for i in distances[1:]]
-    following = lax.ppermute(records[0], "tm", [(i, i - 1) for i in range(1, blocks)])
+    following = lax.ppermute(records[0], "tm", [(i, (i - 1) % blocks) for i in range(blocks)])
     hankel, scale, moves, own_terms = call(
         own_kernel,
         "correlate_own",
@@ -194,13 +199,15 @@
     keep, send = call(functools.partial(early_kernel, distances[1:-1]), "correlate_early", halves, halves)(
         hankel, scale, moves, own_terms, *library[:-1]
     )
-    halves = jax.ShapeDtypeStruct((blocks, own, slab), F32)
-    keep, send = call(functools.partial(last_kernel, distances[-1]), "correlate_last", halves, halves)(
-        hankel, scale, moves, keep, send, library[-1]
-    )
+    last_keep, send = call(
+        functools.partial(last_kernel, distances[-1]),
+        "correlate_last",
+        jax.ShapeDtypeStruct((1, own, slab), F32),
+        jax.ShapeDtypeStruct((blocks, own, slab), F32),
+    )(hankel, scale, moves, send, library[-1])
     arrived = exchange(send, "sta", 1)
     piece = jax.ShapeDtypeStruct((own, slab), F32)
-    chips = call(functools.partial(assemble_kernel, distances), "add_cores", *[piece] * blocks)(keep, arrived)
+    chips = call(functools.partial(assemble_kernel, distances), "add_cores", *[piece] * blocks)(keep, last_keep, arrived)
     others = [exchange(chips[d], "sta", 2 * d) for d in range(blocks - 1, 0, -1)]
     stacked = chips[0]
     for part in others:

time: 25.5 us -> 25.5 us (level)
  starting transfers between devices: 13.1 us -> 11.1 us
  waiting for transfers between devices: 7.91 us -> 9.91 us
    ppermute x1, waiting for transfers between devices: 1.77 us -> 3.07 us  [per_device(): lax.ppermute(records[0], 'tm', [(i, (i - 1) % blocks) for i in range(bloc...]
    ppermute x1, starting transfers between devices: 1.28 us -> 0.01 us  [per_device(): lax.ppermute(records[0], 'tm', [(i, (i - 1) % blocks) for i in range(bloc...]
    ppermute x7, waiting for transfers between devices: 6.15 us -> 6.84 us  [exchange(): lax.ppermute(block, axis, [(i, i ^ distance) for i in range(lax.axis_size...]
    ppermute x7, starting transfers between devices: 11.8 us -> 11.1 us  [exchange(): lax.ppermute(block, axis, [(i, i ^ distance) for i in range(lax.axis_size...]
where the time goes in v6:
time: 25.5 us; the launch traced here: 25.4 us
  starting transfers between devices  11.1 us (44%)
  waiting for transfers between devices  9.91 us (39%)
  Pallas kernels  2.71 us (11%)
  local copies, waits for them, and re-layouts  0.92 us (4%)
  other arithmetic  0.65 us (3%)
    ppermute x7, starting transfers between devices, exchange(): lax.ppermute(block, axis, [(i, i ^ distance) for i in range(lax.axis_size...  11.1 us
    ppermute x7, waiting for transfers between devices, exchange(): lax.ppermute(block, axis, [(i, i ^ distance) for i in range(lax.axis_size...  6.84 us
    ppermute x1, waiting for transfers between devices, per_device(): lax.ppermute(records[0], 'tm', [(i, (i - 1) % blocks) for i in range(bloc...  3.07 us
    pallas_call x1, Pallas kernels, per_device(): call(own_kernel, 'correlate_own', jax.ShapeDtypeStruct((3, TAPS_PAD, reac...  1.12 us
    unnamed x8, local copies, waits for them, and re-layouts  0.92 us
    pallas_call x1, Pallas kernels, per_device(): call(functools.partial(early_kernel, distances[1:-1]), 'correlate_early',...  0.7 us
    add x1, other arithmetic, per_device(): stacked = stacked + part  0.65 us
    pallas_call x1, Pallas kernels, per_device(): call(functools.partial(last_kernel, distances[-1]), 'correlate_last', jax...  0.54 us
  transfers between devices with their start and end apart: 8, of which 6 were waited for; matrix products, arithmetic and copies ran while one was open for 0% of the time, Pallas kernels for 7%

profile of v6, /device:TPU:0, one launch (start us, length us, event | category | flops | bytes accessed | tf_op | source)
XLA Modules:
  0.0 25.4 jit_solution(14508211080625849102)
XLA Ops:
  0.0 0.0 copy-start.1
  0.0 0.0 copy-start
  0.0 0.0 copy-start.2
  0.0 0.0 copy-start.3
  0.0 0.7 %copy-done.1 = s32[1,3,64]{2,0,1:T(1,128)S(1)} copy-done((s32[1,3,64]{2,0,1:T(1,128)S(1)}, s32[1,3,64]{2,0,1:T(1,128)}, u32[]{:S(2)}) %copy-start.1) | copy-done | bytes 792
  0.7 0.2 copy-done
  0.9 0.3 %shape_templates.1.packed_ref = bf16[480,128]{1,0:T(8,128)(2,1)S(1)} custom-call(f32[64,64]{1,0:T(8,128)S(1)} %table.1.table_ref, bf16[3,64,300]{2,1,0:T(8,128)(2,1)S(1)} %bitcast.3, s32[3,1,64]{2,1,0:T(1,128)S(1)} %bitcast.4), custom_call_target="tpu_custom_call" | custom-call | flops 1000 | tf_op jit(solution)/shard_map/shape_templates/pallas_call | solution.py:184
  1.2 4.1 %collective-permute-start.2 = (bf16[480,128]{1,0:T(8,128)(2,1)S(1)}, bf16[480,128]{1,0:T(8,128)(2,1)S(1)}, u32[]{:S(2)}, u32[]{:S(2)}) collective-permute-start(bf16[480,128]{1,0:T(8,128)(2,1)S(1)} %shape_templates.1.packed_ref), channel_id=1, source_target_pairs={{0,2},{1,3},{2,0},{3,1},{4,6},{5,7},{6,4},{7,5},{8,10},{9,11},{10,... | collective-permute-start | bytes 368648 | tf_op jit(solution)/shard_map/ppermute | solution.py:167
  5.3 1.6 %collective-permute-start.1 = (bf16[480,128]{1,0:T(8,128)(2,1)S(1)}, bf16[480,128]{1,0:T(8,128)(2,1)S(1)}, u32[]{:S(2)}, u32[]{:S(2)}) collective-permute-start(bf16[480,128]{1,0:T(8,128)(2,1)S(1)} %shape_templates.1.packed_ref), channel_id=1, source_target_pairs={{0,1},{1,0},{2,3},{3,2},{4,5},{5,4},{6,7},{7,6},{8,9},{9,8},{10,11... | collective-permute-start | bytes 368648 | tf_op jit(solution)/shard_map/ppermute | solution.py:167
  6.9 0.0 copy-done.2
  6.9 0.0 collective-permute-start
  6.9 1.8 %collective-permute-start.3 = (bf16[480,128]{1,0:T(8,128)(2,1)S(1)}, bf16[480,128]{1,0:T(8,128)(2,1)S(1)}, u32[]{:S(2)}, u32[]{:S(2)}) collective-permute-start(bf16[480,128]{1,0:T(8,128)(2,1)S(1)} %shape_templates.1.packed_ref), channel_id=1, source_target_pairs={{0,3},{1,2},{2,1},{3,0},{4,7},{5,6},{6,5},{7,4},{8,11},{9,10},{10,... | collective-permute-start | bytes 368648 | tf_op jit(solution)/shard_map/ppermute | solution.py:167
  8.7 3.1 %collective-permute-done.following_ref = bf16[3,512]{1,0:T(4,128)(2,1)S(1)} collective-permute-done((bf16[3,512]{1,0:T(4,128)(2,1)S(1)}, bf16[3,512]{1,0:T(4,128)(2,1)S(1)}, u32[]{:S(2)}, u32[]{:S(2)}) %collective-permute-start) | collective-permute-done | bytes 3104 | tf_op jit(solution)/shard_map/ppermute | solution.py:189
  11.7 0.0 copy-done.3
  11.8 1.1 %correlate_own.1 = (bf16[3,384,768]{2,1,0:T(8,128)(2,1)S(1)}, f32[3,768]{1,0:T(4,128)S(1)}, s32[1,256]{1,0:T(1,128)S(1)}, f32[64,512]{1,0:T(8,128)S(1)}) custom-call(bf16[3,512]{1,0:T(4,128)(2,1)S(1)} %bitcast.6, bf16[3,512]{1,0:T(4,128)(2,1)S(1)} %collective-permute-done.following_ref, s32[1,256]{1,0:T(1,128)S(1)} %copy-done.3, ...), custom_call_target="tpu_custom_call" | custom-call | flops 1000000000 | tf_op jit(solution)/shard_map/correlate_own/pallas_call | solution.py:190
  12.9 0.0 collective-permute-done.2.refs_1_
  12.9 0.0 collective-permute-done.1.refs_0_
  12.9 0.7 %correlate_early.1 = (f32[3,32,512]{2,1,0:T(8,128)S(1)}, f32[3,32,512]{2,1,0:T(8,128)S(1)}) custom-call(bf16[3,384,768]{2,1,0:T(8,128)(2,1)S(1)} %get-tuple-element.17.hankel_ref, f32[3,768]{1,0:T(4,128)S(1)} %get-tuple-element.18.scale_ref, s32[1,256]{1,0:T(1,128)S(1)} %get-tuple-element.19.moves_ref, f32[64,512]{1,0:T(8,128)S(1)} %get-tuple-element.20.own_ref, ...), custom_call_target="tpu_custom_call" | custom-call | flops 1000000000 | tf_op jit(solution)/shard_map/correlate_early/pallas_call | solution.py:199
  13.6 1.6 %collective-permute-done.3.packed_ref = bf16[480,128]{1,0:T(8,128)(2,1)S(1)} collective-permute-done((bf16[480,128]{1,0:T(8,128)(2,1)S(1)}, bf16[480,128]{1,0:T(8,128)(2,1)S(1)}, u32[]{:S(2)}, u32[]{:S(2)}) %collective-permute-start.3) | collective-permute-done | bytes 122912 | tf_op jit(solution)/shard_map/ppermute | solution.py:167
  15.2 0.5 %correlate_last.1 = (f32[1,32,512]{2,1,0:T(8,128)S(1)}, f32[4,32,512]{2,1,0:T(8,128)S(1)}) custom-call(bf16[3,384,768]{2,1,0:T(8,128)(2,1)S(1)} %get-tuple-element.17.hankel_ref, f32[3,768]{1,0:T(4,128)S(1)} %get-tuple-element.18.scale_ref, s32[1,256]{1,0:T(1,128)S(1)} %get-tuple-element.19.moves_ref, f32[3,32,512]{2,1,0:T(8,128)S(1)} %get-tuple-element.22.early_send_ref, ...), custom_call_target="tpu_custom_call" | custom-call | flops 1000 | tf_op jit(solution)/shard_map/correlate_last/pallas_call | solution.py:202
  15.7 0.1 collective-permute-start.4
  15.8 1.5 %collective-permute-done.4.arrived_ref = f32[4,32,512]{2,1,0:T(8,128)S(1)} collective-permute-done((f32[4,32,512]{2,1,0:T(8,128)S(1)}, f32[4,32,512]{2,1,0:T(8,128)S(1)}, u32[]{:S(2)}, u32[]{:S(2)}) %collective-permute-start.4) | collective-permute-done | bytes 262176 | tf_op jit(solution)/shard_map/ppermute | solution.py:167
  17.3 0.1 add_cores.1
  17.4 2.5 %collective-permute-start.5 = (f32[32,512]{1,0:T(8,128)S(1)}, f32[32,512]{1,0:T(8,128)S(1)}, u32[]{:S(2)}, u32[]{:S(2)}) collective-permute-start(f32[32,512]{1,0:T(8,128)S(1)} %get-tuple-element.26), channel_id=1, source_target_pairs={{0,24},{4,28},{8,16},{12,20},{16,8},{20,12},{24,0},{28,4},{1,25},{... | collective-permute-start | bytes 196616 | tf_op jit(solution)/shard_map/ppermute | solution.py:167
  19.9 0.5 %collective-permute-start.6 = (f32[32,512]{1,0:T(8,128)S(1)}, f32[32,512]{1,0:T(8,128)S(1)}, u32[]{:S(2)}, u32[]{:S(2)}) collective-permute-start(f32[32,512]{1,0:T(8,128)S(1)} %get-tuple-element.27), channel_id=1, source_target_pairs={{0,16},{4,20},{8,24},{12,28},{16,0},{20,4},{24,8},{28,12},{1,17},{... | collective-permute-start | bytes 196616 | tf_op jit(solution)/shard_map/ppermute | solution.py:167
  20.4 0.5 %collective-permute-start.7 = (f32[32,512]{1,0:T(8,128)S(1)}, f32[32,512]{1,0:T(8,128)S(1)}, u32[]{:S(2)}, u32[]{:S(2)}) collective-permute-start(f32[32,512]{1,0:T(8,128)S(1)} %get-tuple-element.28), channel_id=1, source_target_pairs={{0,8},{4,12},{8,0},{12,4},{16,24},{20,28},{24,16},{28,20},{1,9},{5... | collective-permute-start | bytes 196616 | tf_op jit(solution)/shard_map/ppermute | solution.py:167
  21.0 1.7 %collective-permute-done.5 = f32[32,512]{1,0:T(8,128)S(1)} collective-permute-done((f32[32,512]{1,0:T(8,128)S(1)}, f32[32,512]{1,0:T(8,128)S(1)}, u32[]{:S(2)}, u32[]{:S(2)}) %collective-permute-start.5) | collective-permute-done | bytes 65568 | tf_op jit(solution)/shard_map/ppermute | solution.py:167
  22.7 1.5 %collective-permute-done.6 = f32[32,512]{1,0:T(8,128)S(1)} collective-permute-done((f32[32,512]{1,0:T(8,128)S(1)}, f32[32,512]{1,0:T(8,128)S(1)}, u32[]{:S(2)}, u32[]{:S(2)}) %collective-permute-start.6) | collective-permute-done | bytes 65568 | tf_op jit(solution)/shard_map/ppermute | solution.py:167
  24.2 0.5 %collective-permute-done.7 = f32[32,512]{1,0:T(8,128)S(1)} collective-permute-done((f32[32,512]{1,0:T(8,128)S(1)}, f32[32,512]{1,0:T(8,128)S(1)}, u32[]{:S(2)}, u32[]{:S(2)}) %collective-permute-start.7) | collective-permute-done | bytes 65568 | tf_op jit(solution)/shard_map/ppermute | solution.py:167
  24.7 0.7 %add_add_fusion = f32[32,512]{1,0:T(8,128)} fusion(f32[32,512]{1,0:T(8,128)S(1)} %collective-permute-done.7, f32[32,512]{1,0:T(8,128)S(1)} %collective-permute-done.6, f32[32,512]{1,0:T(8,128)S(1)} %get-tuple-element.25, f32[32,512]{1,0:T(8,128)S(1)} %collective-permute-done.5), kind=kLoop, calls=%fused_computation | loop fusion | flops 49152 | bytes 327680 | tf_op jit(solution)/shard_map/add | solution.py:214
  (1 shorter events, 0.0 us)
Async XLA Ops:
  0.0 0.7 %copy-start.1 = (s32[1,3,64]{2,0,1:T(1,128)S(1)}, s32[1,3,64]{2,0,1:T(1,128)}, u32[]{:S(2)}) copy-start(s32[1,3,64]{2,0,1:T(1,128)} %param.6) | copy-start | bytes 2308
  0.0 0.9 %copy-start = (bf16[1,3,64,300]{3,2,1,0:T(8,128)(2,1)S(1)}, bf16[1,3,64,300]{3,2,1,0:T(8,128)(2,1)}, u32[]{:S(2)}) copy-start(bf16[1,3,64,300]{3,2,1,0:T(8,128)(2,1)} %param.5) | copy-start | bytes 345604
  0.0 6.9 %copy-start.2 = (bf16[1,3,512]{2,1,0:T(4,128)(2,1)S(1)}, bf16[1,3,512]{2,1,0:T(4,128)(2,1)}, u32[]{:S(2)}) copy-start(bf16[1,3,512]{2,1,0:T(4,128)(2,1)} %param.4) | copy-start | bytes 9220
  0.0 11.7 %copy-start.3 = (s32[1,256]{1,0:T(1,128)S(1)}, s32[1,256]{1,0:T(1,128)}, u32[]{:S(2)}) copy-start(s32[1,256]{1,0:T(1,128)} %moves_ref.1) | copy-start | bytes 3076
  1.2 11.7 %collective-permute-start.2 = (bf16[480,128]{1,0:T(8,128)(2,1)S(1)}, bf16[480,128]{1,0:T(8,128)(2,1)S(1)}, u32[]{:S(2)}, u32[]{:S(2)}) collective-permute-start(bf16[480,128]{1,0:T(8,128)(2,1)S(1)} %shape_templates.1.packed_ref), channel_id=1, source_target_pairs={{0,2},{1,3},{2,0},{3,1},{4,6},{5,7},{6,4},{7,5},{8,10},{9,11},{10,... | collective-permute-start | bytes 368648 | tf_op jit(solution)/shard_map/ppermute | solution.py:167
  5.3 7.6 %collective-permute-start.1 = (bf16[480,128]{1,0:T(8,128)(2,1)S(1)}, bf16[480,128]{1,0:T(8,128)(2,1)S(1)}, u32[]{:S(2)}, u32[]{:S(2)}) collective-permute-start(bf16[480,128]{1,0:T(8,128)(2,1)S(1)} %shape_templates.1.packed_ref), channel_id=1, source_target_pairs={{0,1},{1,0},{2,3},{3,2},{4,5},{5,4},{6,7},{7,6},{8,9},{9,8},{10,11... | collective-permute-start | bytes 368648 | tf_op jit(solution)/shard_map/ppermute | solution.py:167
  6.9 4.9 %collective-permute-start = (bf16[3,512]{1,0:T(4,128)(2,1)S(1)}, bf16[3,512]{1,0:T(4,128)(2,1)S(1)}, u32[]{:S(2)}, u32[]{:S(2)}) collective-permute-start(bf16[3,512]{1,0:T(4,128)(2,1)S(1)} %bitcast.5), channel_id=1, source_target_pairs={{0,3},{1,0},{2,1},{3,2},{4,7},{5,4},{6,5},{7,6},{8,11},{9,8},{10,9... | collective-permute-start | bytes 9224 | tf_op jit(solution)/shard_map/ppermute | solution.py:189
  6.9 8.3 %collective-permute-start.3 = (bf16[480,128]{1,0:T(8,128)(2,1)S(1)}, bf16[480,128]{1,0:T(8,128)(2,1)S(1)}, u32[]{:S(2)}, u32[]{:S(2)}) collective-permute-start(bf16[480,128]{1,0:T(8,128)(2,1)S(1)} %shape_templates.1.packed_ref), channel_id=1, source_target_pairs={{0,3},{1,2},{2,1},{3,0},{4,7},{5,6},{6,5},{7,4},{8,11},{9,10},{10,... | collective-permute-start | bytes 368648 | tf_op jit(solution)/shard_map/ppermute | solution.py:167
  15.7 1.6 %collective-permute-start.4 = (f32[4,32,512]{2,1,0:T(8,128)S(1)}, f32[4,32,512]{2,1,0:T(8,128)S(1)}, u32[]{:S(2)}, u32[]{:S(2)}) collective-permute-start(f32[4,32,512]{2,1,0:T(8,128)S(1)} %get-tuple-element.24), channel_id=1, source_target_pairs={{0,4},{4,0},{8,12},{12,8},{16,20},{20,16},{24,28},{28,24},{1,5},{5... | collective-permute-start | bytes 786440 | tf_op jit(solution)/shard_map/ppermute | solution.py:167
  17.4 5.3 %collective-permute-start.5 = (f32[32,512]{1,0:T(8,128)S(1)}, f32[32,512]{1,0:T(8,128)S(1)}, u32[]{:S(2)}, u32[]{:S(2)}) collective-permute-start(f32[32,512]{1,0:T(8,128)S(1)} %get-tuple-element.26), channel_id=1, source_target_pairs={{0,24},{4,28},{8,16},{12,20},{16,8},{20,12},{24,0},{28,4},{1,25},{... | collective-permute-start | bytes 196616 | tf_op jit(solution)/shard_map/ppermute | solution.py:167
  19.9 4.3 %collective-permute-start.6 = (f32[32,512]{1,0:T(8,128)S(1)}, f32[32,512]{1,0:T(8,128)S(1)}, u32[]{:S(2)}, u32[]{:S(2)}) collective-permute-start(f32[32,512]{1,0:T(8,128)S(1)} %get-tuple-element.27), channel_id=1, source_target_pairs={{0,16},{4,20},{8,24},{12,28},{16,0},{20,4},{24,8},{28,12},{1,17},{... | collective-permute-start | bytes 196616 | tf_op jit(solution)/shard_map/ppermute | solution.py:167
  20.4 4.3 %collective-permute-start.7 = (f32[32,512]{1,0:T(8,128)S(1)}, f32[32,512]{1,0:T(8,128)S(1)}, u32[]{:S(2)}, u32[]{:S(2)}) collective-permute-start(f32[32,512]{1,0:T(8,128)S(1)} %get-tuple-element.28), channel_id=1, source_target_pairs={{0,8},{4,12},{8,0},{12,4},{16,24},{20,28},{24,16},{28,20},{1,9},{5... | collective-permute-start | bytes 196616 | tf_op jit(solution)/shard_map/ppermute | solution.py:167
